TPU v7x, 32 devices: a whole 2x2x4 slice. The times are simulated.
32 devices in a mesh: row: 4 (over z), col: 8 (over y, x, core).
Axes of the slice: x: 2, y: 2, z: 4, core: 2. Of those that a mesh axis runs over, the one named last changes fastest.
Arguments:
- layer_input: bfloat16 [2, 4, 1024, 1792], P(None, 'row', 'col'), may hold values from -6 to 6
- cotangent: bfloat16 [2, 4, 1024, 1792], P(None, 'row', 'col'), may hold values from -6 to 6
- segments: int32 [2, 4, 1024], P(None, 'row'), may hold values from 0 to 1, never falling along the last dimension, each value on 1 to 768 neighbouring positions
- norm_gains: float32 [2, 1792], replicated, may hold values from 0.5 to 1.5
- gain_mean: float32 [2, 1792], replicated, may hold values from -56 to 56
- gain_square: float32 [2, 1792], replicated, may hold values from 409.6 to 1638.4
- conv_kernel: float32 [3, 1792], P(None, 'col'), may hold values from -4 to 4
- conv_mean: float32 [3, 1792], P(None, 'col'), may hold values from -56 to 56
- conv_square: float32 [3, 1792], P(None, 'col'), may hold values from 409.6 to 1638.4
- mix_weight: float32 [1792, 16, 256], P('row', 'col'), may hold values from -0.125 to 0.125
- mix_mean: float32 [1792, 16, 256], P('row', 'col'), may hold values from -56 to 56
- mix_square: float32 [1792, 16, 256], P('row', 'col'), may hold values from 409.6 to 1638.4
- out_weight: float32 [1792, 1792], P('col', 'row'), may hold values from -1 to 1
- out_mean: float32 [1792, 1792], P('col', 'row'), may hold values from -6 to 6
- out_square: float32 [1792, 1792], P('col', 'row'), may hold values from 1.6 to 6.4
- up_weight: float32 [2, 4864, 1792], P(None, ('row', 'col')), may hold values from -0.125 to 0.125
- up_mean: float32 [2, 4864, 1792], P(None, ('row', 'col')), may hold values from -20 to 20
- up_square: float32 [2, 4864, 1792], P(None, ('row', 'col')), may hold values from 49.152 to 196.608
- down_weight: float32 [4864, 1792], P(('row', 'col')), may hold values from -0.078125 to 0.078125
- down_mean: float32 [4864, 1792], P(('row', 'col')), may hold values from -32 to 32
- down_square: float32 [4864, 1792], P(('row', 'col')), may hold values from 147.456 to 589.824
Outputs:
- layer_output: bfloat16 [2, 4, 1024, 1792], P(None, 'row', 'col')
- input_grad: float32 [2, 4, 1024, 1792], P(None, 'row', 'col')
- gain_means: float32 [2, 1792], replicated
- gain_squares: float32 [2, 1792], replicated
- new_gains: float32 [2, 1792], replicated
- conv_means: float32 [3, 1792], P(None, 'col')
- conv_squares: float32 [3, 1792], P(None, 'col')
- new_kernel: float32 [3, 1792], P(None, 'col')
- mix_means: float32 [1792, 16, 256], P('row', 'col')
- mix_squares: float32 [1792, 16, 256], P('row', 'col')
- new_mix: float32 [1792, 16, 256], P('row', 'col')
- mix_copy: bfloat16 [1792, 16, 256], P('row', 'col')
- out_means: float32 [1792, 1792], P('col', 'row')
- out_squares: float32 [1792, 1792], P('col', 'row')
- new_out: float32 [1792, 1792], P('col', 'row')
- out_copy: bfloat16 [1792, 1792], P('col', 'row')
- up_means: float32 [2, 4864, 1792], P(None, ('row', 'col'))
- up_squares: float32 [2, 4864, 1792], P(None, ('row', 'col'))
- new_up: float32 [2, 4864, 1792], P(None, ('row', 'col'))
- up_copy: bfloat16 [2, 4864, 1792], P(None, ('row', 'col'))
- down_means: float32 [4864, 1792], P(('row', 'col'))
- down_squares: float32 [4864, 1792], P(('row', 'col'))
- new_down: float32 [4864, 1792], P(('row', 'col'))
- down_copy: bfloat16 [4864, 1792], P(('row', 'col'))
Inputs may be any that keep to these rules, and one draw needn't show every extreme that they name: `segments`: along each sequence the document numbers never fall; each document holds 1 to 768 tokens.
All inputs are finite; a program needn't handle non-finite values.
Results may differ from a plain program's by a relative error of at most 0.025.
Values may be sent and summed in bfloat16 or wider, within the bound.
No kernel may reach another device: no remote copies, remote signals or barrier semaphores. Data moves between devices by JAX's collectives and lax.ppermute only.
A program may use at most 256 MiB of HBM per device.

v0:
```python
import math

import jax
import jax.numpy as jnp
from jax import lax
from jax.sharding import PartitionSpec as P

D = 1792
FF = 4864
STEP = 10


NORM_EPSILON = 1e-05
BETA_ONE = 0.9
BETA_TWO = 0.95
ADAM_EPSILON = 1e-08
DECAY_RATE = 0.1
VECTOR_RATE = 0.5


def silu_grad(tensor):
    sigmoid_val = jax.nn.sigmoid(tensor)
    return sigmoid_val * (1.0 + tensor * (1.0 - sigmoid_val))


def shift_down(tensor, offset):
    filler = jnp.zeros((offset,) + tensor.shape[1:], tensor.dtype)
    return jnp.concatenate([filler, tensor[: tensor.shape[0] - offset]], axis=0)


def shift_up(tensor, offset):
    filler = jnp.zeros((offset,) + tensor.shape[1:], tensor.dtype)
    return jnp.concatenate([tensor[offset:], filler], axis=0)


def same_segment(segs, offset):
    earlier = jnp.concatenate([jnp.full((offset,), -1, jnp.int32), segs[: segs.shape[0] - offset]])
    return (earlier == segs).astype(jnp.float32)


def contract_rows(left_side, right_side):
    return lax.dot_general(
        left_side, right_side, (((0,), (0,)), ((), ())), preferred_element_type=jnp.float32
    )


def contract_cols(left_side, right_side):
    return lax.dot_general(
        left_side, right_side, (((1,), (1,)), ((), ())), preferred_element_type=jnp.float32
    )


def row_scale(tensor):
    return lax.rsqrt(jnp.mean(tensor * tensor, axis=1, keepdims=True) + NORM_EPSILON)


def adam_update(weight, gradient, moment_one, moment_two, step_rate, decay_rate):
    first_new = BETA_ONE * moment_one + (1.0 - BETA_ONE) * gradient
    second_new = BETA_TWO * moment_two + (1.0 - BETA_TWO) * gradient * gradient
    first_hat = first_new / (1.0 - BETA_ONE**STEP)
    second_hat = second_new / (1.0 - BETA_TWO**STEP)
    weight_new = weight - step_rate * (
        first_hat / (jnp.sqrt(second_hat) + ADAM_EPSILON) + decay_rate * weight
    )
    return (first_new, second_new, weight_new)


def local(
    layer_input,
    cotangent,
    segments,
    norm_gains,
    gain_mean,
    gain_square,
    conv_kernel,
    conv_mean,
    conv_square,
    mix_weight,
    mix_mean,
    mix_square,
    out_weight,
    out_mean,
    out_square,
    up_weight,
    up_mean,
    up_square,
    down_weight,
    down_mean,
    down_square,
):
    length = segments.shape[2]
    width_all = layer_input.shape[3]
    heads_here = mix_weight.shape[1]
    pack_dim = mix_weight.shape[2]
    width_col = out_weight.shape[0]
    head_dim = width_col // heads_here
    feat_dim = (pack_dim - 2 * head_dim) // 2
    tap_count = conv_kernel.shape[0]
    row_count = lax.axis_size("row")
    hidden_col = down_weight.shape[0] * row_count
    block_rows = min(512, length)
    block_count = length // block_rows
    feat_root = math.sqrt(feat_dim)
    positions = jnp.arange(length, dtype=jnp.int32)
    kernel_taps = conv_kernel.reshape(tap_count, heads_here, head_dim)

    def fetch_weights():
        mix_full, out_full, up_full, down_full = (
            lax.all_gather(mix_weight.astype(jnp.bfloat16), "row", axis=0, tiled=True),
            lax.all_gather(out_weight.astype(jnp.bfloat16), "row", axis=1, tiled=True),
            lax.all_gather(up_weight.astype(jnp.bfloat16), "row", axis=1, tiled=True),
            lax.all_gather(down_weight.astype(jnp.bfloat16), "row", axis=0, tiled=True),
        )
        return (
            mix_full.reshape(width_all, heads_here * pack_dim),
            out_full,
            up_full.reshape(2 * hidden_col, width_all),
            down_full,
        )

    def micro_step(running, batch_item):
        mix_full, out_full, up_flat, down_full = fetch_weights()
        input_part = batch_item[0][0]
        cot_part = batch_item[1][0]
        segs = batch_item[2][0]
        input_col = input_part.astype(jnp.float32)
        input_full = lax.all_gather(input_part, "col", axis=0, tiled=True).astype(jnp.float32)
        scale_one = row_scale(input_full)
        norm_one = input_full * scale_one * norm_gains[0]
        normed = norm_one.astype(jnp.bfloat16)
        scale_one_col = row_scale(input_col)
        norm_one_col = input_col * scale_one_col * norm_gains[0]
        projected = jnp.dot(normed, mix_full, preferred_element_type=jnp.float32).reshape(
            length, heads_here, pack_dim
        )
        queries = projected[:, :, :feat_dim].astype(jnp.bfloat16)
        key_rows = projected[:, :, feat_dim : 2 * feat_dim].astype(jnp.bfloat16)
        inner_vals = projected[:, :, 2 * feat_dim : 2 * feat_dim + head_dim]
        gate_mix = projected[:, :, 2 * feat_dim + head_dim :]
        seg_links = [same_segment(segs, offset)[:, None, None] for offset in range(tap_count)]
        convolved = kernel_taps[0] * inner_vals
        for offset in range(1, tap_count):
            convolved = (
                convolved + kernel_taps[offset] * shift_down(inner_vals, offset) * seg_links[offset]
            )
        gate_act = gate_mix * jax.nn.sigmoid(gate_mix)
        values = (convolved * gate_act).astype(jnp.bfloat16)

        def scores_of(first_row):
            query_block = lax.dynamic_slice_in_dim(queries, first_row, block_rows, 0)
            seg_block = lax.dynamic_slice_in_dim(segs, first_row, block_rows, 0)
            pos_block = first_row + jnp.arange(block_rows, dtype=jnp.int32)
            scores = (
                jnp.einsum(
                    "thf,rhf->htr", query_block, key_rows, preferred_element_type=jnp.float32
                )
                / feat_root
            )
            key_mask = (pos_block[:, None] >= positions[None, :]) & (
                seg_block[:, None] == segs[None, :]
            )
            kern = jnp.where(key_mask[None], 1.0 + scores + 0.5 * scores * scores, 0.0)
            return (query_block, scores, key_mask, kern)

        def forward_block(block_index):
            query_block, scores, key_mask, kern = scores_of(block_index * block_rows)
            row_total = jnp.sum(kern, axis=2)
            weights = (kern / row_total[:, :, None]).astype(jnp.bfloat16)
            out_block = jnp.einsum(
                "htr,rhe->the", weights, values, preferred_element_type=jnp.float32
            )
            return (out_block.astype(jnp.bfloat16), row_total)

        out_blocks, row_totals = lax.map(forward_block, jnp.arange(block_count, dtype=jnp.int32))
        attended = out_blocks.reshape(length, width_col)
        partial_mix = jnp.dot(attended, out_full, preferred_element_type=jnp.float32)
        mixer_sum = lax.psum_scatter(
            partial_mix.astype(jnp.bfloat16), "col", scatter_dimension=0, tiled=True
        ).astype(jnp.float32)
        resid_col = input_col + mixer_sum
        resid_full = lax.all_gather(
            resid_col.astype(jnp.bfloat16), "col", axis=0, tiled=True
        ).astype(resid_col.dtype)
        scale_two = row_scale(resid_full)
        norm_two = resid_full * scale_two * norm_gains[1]
        normed_two = norm_two.astype(jnp.bfloat16)
        scale_two_col = row_scale(resid_col)
        norm_two_col = resid_col * scale_two_col * norm_gains[1]
        gate_up = contract_cols(normed_two, up_flat).reshape(length, 2, hidden_col)
        gate_val = gate_up[:, 0]
        up_val = gate_up[:, 1]
        gate_sig = gate_val * jax.nn.sigmoid(gate_val)
        hidden = (gate_sig * up_val).astype(jnp.bfloat16)
        partial_ffn = jnp.dot(hidden, down_full, preferred_element_type=jnp.float32)
        ffn_sum = lax.psum_scatter(
            partial_ffn.astype(jnp.bfloat16), "col", scatter_dimension=0, tiled=True
        ).astype(jnp.float32)
        output = (resid_col + ffn_sum).astype(jnp.bfloat16)
        cot_full = lax.all_gather(cot_part, "col", axis=0, tiled=True)
        cot_col = cot_part.astype(jnp.float32)
        grad_hidden = contract_cols(cot_full, down_full)
        grad_down = contract_rows(hidden, cot_full)
        grad_gate = grad_hidden * up_val * silu_grad(gate_val)
        grad_upval = grad_hidden * gate_sig
        grad_gu = (
            jnp.stack([grad_gate, grad_upval], axis=1)
            .reshape(length, 2 * hidden_col)
            .astype(jnp.bfloat16)
        )
        grad_up = contract_rows(grad_gu, normed_two)
        back_two = jnp.dot(grad_gu, up_flat, preferred_element_type=jnp.float32)
        back_col = lax.psum_scatter(
            back_two.astype(jnp.bfloat16), "col", scatter_dimension=0, tiled=True
        ).astype(jnp.float32)
        mean_two = jnp.mean(back_col * norm_two_col, axis=1, keepdims=True)
        resid_grad = cot_col + scale_two_col * (
            norm_gains[1] * back_col - resid_col * scale_two_col * mean_two
        )
        resid_low = lax.all_gather(resid_grad.astype(jnp.bfloat16), "col", axis=0, tiled=True)
        gain_two = jnp.sum(back_col * resid_col * scale_two_col, axis=0)
        grad_out = contract_rows(attended, resid_low)
        grad_att = (
            contract_cols(resid_low, out_full)
            .astype(jnp.bfloat16)
            .reshape(length, heads_here, head_dim)
        )

        def backward_block(sums_kv, block_index):
            grad_keys, grad_values = sums_kv
            first_row = block_index * block_rows
            query_block, scores, key_mask, kern = scores_of(first_row)
            row_total = row_totals[block_index]
            probabilities = kern / row_total[:, :, None]
            weights = probabilities.astype(jnp.bfloat16)
            grad_block = lax.dynamic_slice_in_dim(grad_att, first_row, block_rows, 0)
            grad_probs = jnp.einsum(
                "the,rhe->htr", grad_block, values, preferred_element_type=jnp.float32
            )
            row_dot = jnp.sum(grad_probs * probabilities, axis=2, keepdims=True)
            grad_kern = (grad_probs - row_dot) / row_total[:, :, None]
            grad_scores = jnp.where(key_mask[None], grad_kern * (1.0 + scores), 0.0).astype(
                jnp.bfloat16
            )
            grad_query_block = (
                jnp.einsum(
                    "htr,rhf->thf", grad_scores, key_rows, preferred_element_type=jnp.float32
                )
                / feat_root
            )
            grad_keys = (
                grad_keys
                + jnp.einsum(
                    "htr,thf->rhf", grad_scores, query_block, preferred_element_type=jnp.float32
                )
                / feat_root
            )
            grad_values = grad_values + jnp.einsum(
                "htr,the->rhe", weights, grad_block, preferred_element_type=jnp.float32
            )
            return ((grad_keys, grad_values), grad_query_block)

        start_sums = (
            jnp.zeros((length, heads_here, feat_dim), jnp.float32),
            jnp.zeros((length, heads_here, head_dim), jnp.float32),
        )
        (grad_keys, grad_values), grad_queries = lax.scan(
            backward_block, start_sums, jnp.arange(block_count, dtype=jnp.int32)
        )
        grad_queries = grad_queries.reshape(length, heads_here, feat_dim)
        grad_conv_out = grad_values * gate_act
        grad_gate_mix = grad_values * convolved * silu_grad(gate_mix)
        grad_inner = kernel_taps[0] * grad_conv_out
        conv_grads = [jnp.sum(grad_conv_out * inner_vals, axis=0).reshape(width_col)]
        for offset in range(1, tap_count):
            masked = grad_conv_out * seg_links[offset]
            grad_inner = grad_inner + kernel_taps[offset] * shift_up(masked, offset)
            conv_grads.append(
                jnp.sum(masked * shift_down(inner_vals, offset), axis=0).reshape(width_col)
            )
        grad_proj = jnp.concatenate([grad_queries, grad_keys, grad_inner, grad_gate_mix], axis=2)
        grad_proj = grad_proj.astype(jnp.bfloat16).reshape(length, heads_here * pack_dim)
        grad_mix = contract_rows(normed, grad_proj)
        back_one = contract_cols(grad_proj, mix_full)
        back_one_col = lax.psum_scatter(
            back_one.astype(jnp.bfloat16), "col", scatter_dimension=0, tiled=True
        ).astype(jnp.float32)
        mean_one = jnp.mean(back_one_col * norm_one_col, axis=1, keepdims=True)
        grad_input = resid_grad + scale_one_col * (
            norm_gains[0] * back_one_col - input_col * scale_one_col * mean_one
        )
        gain_one = jnp.sum(back_one_col * input_col * scale_one_col, axis=0)
        gain_grads = jnp.stack([gain_one, gain_two], axis=0)
        tap_grads = jnp.stack(conv_grads, axis=0)
        sum_mix, sum_out, sum_up, sum_down, sum_gains, sum_taps = running
        running = (
            sum_mix + grad_mix,
            sum_out + grad_out,
            sum_up + grad_up,
            sum_down + grad_down,
            sum_gains + gain_grads,
            sum_taps + tap_grads,
        )
        return (running, (output[None], grad_input[None]))

    zero_sums = (
        jnp.zeros((width_all, heads_here * pack_dim), jnp.float32),
        jnp.zeros((width_col, width_all), jnp.float32),
        jnp.zeros((2 * hidden_col, width_all), jnp.float32),
        jnp.zeros((hidden_col, width_all), jnp.float32),
        jnp.zeros((2, width_all), jnp.float32),
        jnp.zeros((tap_count, width_col), jnp.float32),
    )
    grad_sums, (outputs, grads_input) = lax.scan(
        micro_step, zero_sums, (layer_input, cotangent, segments)
    )
    sum_mix, sum_out, sum_up, sum_down, sum_gains, sum_taps = grad_sums
    conv_wide = jnp.broadcast_to(sum_taps[None], (row_count, tap_count, width_col))
    red_mix, red_out, red_up, red_down, red_conv = (
        lax.psum_scatter(
            sum_mix.astype(jnp.bfloat16), "row", scatter_dimension=0, tiled=True
        ).astype(jnp.float32),
        lax.psum_scatter(
            sum_out.astype(jnp.bfloat16), "row", scatter_dimension=1, tiled=True
        ).astype(jnp.float32),
        lax.psum_scatter(
            sum_up.reshape(2, hidden_col, width_all).astype(jnp.bfloat16),
            "row",
            scatter_dimension=1,
            tiled=True,
        ).astype(jnp.float32),
        lax.psum_scatter(
            sum_down.astype(jnp.bfloat16), "row", scatter_dimension=0, tiled=True
        ).astype(jnp.float32),
        lax.psum_scatter(
            conv_wide.astype(jnp.bfloat16), "row", scatter_dimension=0, tiled=True
        ).astype(jnp.float32),
    )
    red_gains = lax.psum(sum_gains, ("row", "col"))
    red_mix = red_mix.reshape(mix_weight.shape)
    red_conv = red_conv[0]
    gain_means, gain_squares, new_gains = adam_update(
        norm_gains, red_gains, gain_mean, gain_square, VECTOR_RATE, 0.0
    )
    conv_means, conv_squares, new_kernel = adam_update(
        conv_kernel, red_conv, conv_mean, conv_square, VECTOR_RATE, 0.0
    )
    mix_means, mix_squares, new_mix = adam_update(
        mix_weight, red_mix, mix_mean, mix_square, D ** (-0.5), DECAY_RATE
    )
    out_means, out_squares, new_out = adam_update(
        out_weight, red_out, out_mean, out_square, 8.0 * D ** (-0.5), DECAY_RATE
    )
    up_means, up_squares, new_up = adam_update(
        up_weight, red_up, up_mean, up_square, D ** (-0.5), DECAY_RATE
    )
    down_means, down_squares, new_down = adam_update(
        down_weight, red_down, down_mean, down_square, FF ** (-0.5), DECAY_RATE
    )
    return (
        outputs,
        grads_input,
        gain_means,
        gain_squares,
        new_gains,
        conv_means,
        conv_squares,
        new_kernel,
        mix_means,
        mix_squares,
        new_mix,
        new_mix.astype(jnp.bfloat16),
        out_means,
        out_squares,
        new_out,
        new_out.astype(jnp.bfloat16),
        up_means,
        up_squares,
        new_up,
        new_up.astype(jnp.bfloat16),
        down_means,
        down_squares,
        new_down,
        new_down.astype(jnp.bfloat16),
    )


def solution(mesh):
    placed = (
        P(None, "row", "col", None),
        P(None, "row", "col", None),
        P(None, "row", None),
        P(),
        P(),
        P(),
        P(None, "col"),
        P(None, "col"),
        P(None, "col"),
        P("row", "col", None),
        P("row", "col", None),
        P("row", "col", None),
        P("col", "row"),
        P("col", "row"),
        P("col", "row"),
        P(None, ("row", "col"), None),
        P(None, ("row", "col"), None),
        P(None, ("row", "col"), None),
        P(("row", "col"), None),
        P(("row", "col"), None),
        P(("row", "col"), None),
    )
    return jax.shard_map(
        local,
        mesh=mesh,
        in_specs=placed,
        out_specs=(
            P(None, "row", "col", None),
            P(None, "row", "col", None),
            P(),
            P(),
            P(),
            P(None, "col"),
            P(None, "col"),
            P(None, "col"),
            P("row", "col", None),
            P("row", "col", None),
            P("row", "col", None),
            P("row", "col", None),
            P("col", "row"),
            P("col", "row"),
            P("col", "row"),
            P("col", "row"),
            P(None, ("row", "col"), None),
            P(None, ("row", "col"), None),
            P(None, ("row", "col"), None),
            P(None, ("row", "col"), None),
            P(("row", "col"), None),
            P(("row", "col"), None),
            P(("row", "col"), None),
            P(("row", "col"), None),
        ),
        check_vma=False,
    )
```

profile of v0, /device:TPU:0, one launch (start us, length us, event | category | flops | bytes accessed | tf_op | source)
XLA Modules:
  0.0 1443.0 jit_solution(15951859776495910118)
XLA Ops:
  17.0 1208.9 %while.93 = (s32[]{:T(128)}, f32[1792,512]{1,0:T(8,128)}, f32[224,1792]{1,0:T(8,128)}, f32[1216,1792]{1,0:T(8,128)}, f32[608,1792]{1,0:T(8,128)}, /*index=5*/f32...) while((s32[]{:T(128)}, f32[1792,512]{1,0:T(8,128)}, ...), condition=%wide.region_22.23_spmd.clone.clone, body=%wide.region_0.22_spmd.clone.clone.sunk | while | flops 29889136640 | bytes 564635776 | solution.py:313
  22.7 33.0 %all_gather.78 = bf16[224,1792]{0,1:T(8,128)(2,1)S(1)} all-gather(bf16[224,448]{0,1:T(8,128)(2,1)S(1)} %get-tuple-element.1505), channel_id=1, replica_groups=mesh['row'=4,'col'=8] {'row'}, dimensions={1}, use_global_device_ids=true | all-gather | bytes 1003520 | tf_op jit(solution)/shard_map/while/body/eval_jaxpr/all_gather | solution.py:110
  77.7 32.8 %all-gather.18.cloned.1.call-done = bf16[1,1,1024,1792]{3,2,1,0:T(8,128)(2,1)} async-done(((bf16[1,1,128,1792]{3,2,1,0:T(8,128)(2,1)}), bf16[1,1,1024,1792]{3,2,1,0:T(8,128)(2,1)}) %all-gather.18.cloned.1.call-update) | async-done | bytes 3670032 | tf_op jit(solution)/shard_map/while/body/eval_jaxpr/all_gather | solution.py:127
  137.2 48.8 %reduce-scatter.21.cloned.1.call-done = bf16[128,1792]{1,0:T(8,128)(2,1)} async-done(((bf16[1024,1792]{1,0:T(8,128)(2,1)}), bf16[128,1792]{1,0:T(8,128)(2,1)}) %reduce-scatter.21.cloned.1.call-update) | async-done | bytes 458768 | tf_op jit(solution)/shard_map/while/body/eval_jaxpr/reduce_scatter | solution.py:177
  190.3 32.6 %all-gather.22.cloned.1.call-done = bf16[1024,1792]{1,0:T(8,128)(2,1)} async-done(((bf16[128,1792]{1,0:T(8,128)(2,1)}), bf16[1024,1792]{1,0:T(8,128)(2,1)}) %all-gather.22.cloned.1.call-update) | async-done | bytes 3670032 | tf_op jit(solution)/shard_map/while/body/eval_jaxpr/all_gather | solution.py:181
  225.7 82.6 %all-gather.20.cloned.1.call-done = bf16[2,608,1792]{2,1,0:T(8,128)(2,1)} async-done(((bf16[2,152,1792]{2,1,0:T(8,128)(2,1)}), bf16[2,608,1792]{2,1,0:T(8,128)(2,1)}) %all-gather.20.cloned.1.call-update) | async-done | bytes 4358160 | tf_op jit(solution)/shard_map/while/body/eval_jaxpr/all_gather | solution.py:111
  318.9 37.6 %all-gather.24.cloned.1.call-done = bf16[608,1792]{1,0:T(8,128)(2,1)} async-done(((bf16[152,1792]{1,0:T(8,128)(2,1)}), bf16[608,1792]{1,0:T(8,128)(2,1)}) %all-gather.24.cloned.1.call-update) | async-done | bytes 2179088 | tf_op jit(solution)/shard_map/while/body/eval_jaxpr/all_gather | solution.py:112
  356.4 35.8 %all-gather.26.cloned.1.call-done = bf16[1,1,1024,1792]{3,2,1,0:T(8,128)(2,1)} async-done(((bf16[1,1,128,1792]{3,2,1,0:T(8,128)(2,1)}), bf16[1,1,1024,1792]{3,2,1,0:T(8,128)(2,1)}) %all-gather.26.cloned.1.call-update) | async-done | bytes 3670032 | tf_op jit(solution)/shard_map/while/body/eval_jaxpr/all_gather | solution.py:199
  407.9 48.8 %reduce-scatter.23.cloned.1.call-done = bf16[128,1792]{1,0:T(8,128)(2,1)} async-done(((bf16[1024,1792]{1,0:T(8,128)(2,1)}), bf16[128,1792]{1,0:T(8,128)(2,1)}) %reduce-scatter.23.cloned.1.call-update) | async-done | bytes 458768 | tf_op jit(solution)/shard_map/while/body/eval_jaxpr/reduce_scatter | solution.py:212
  470.4 25.3 %all-gather.28.cloned.1.call-done = bf16[1024,1792]{1,0:T(8,128)(2,1)} async-done(((bf16[128,1792]{1,0:T(8,128)(2,1)}), bf16[1024,1792]{1,0:T(8,128)(2,1)}) %all-gather.28.cloned.1.call-update) | async-done | bytes 3670032 | tf_op jit(solution)/shard_map/while/body/eval_jaxpr/all_gather | solution.py:219
  499.9 56.0 %while.95 = (s32[]{:T(128)}, f32[1024,2,16]{0,2,1:T(8,128)S(1)}, f32[1024,2,112]{0,2,1:T(8,128)}, bf16[2,512,2,16]{1,0,3,2:T(2,128)(2,1)S(1)}, s32[2]{0:T(128)S(...) while((s32[]{:T(128)}, f32[1024,2,16]{0,2,1:T(8,128)S(1)}, ...), condition=%wide.region_12.12_spmd.clone, body=%wide.region_10.11_spmd.clone.sunk | while | flops 1317081600 | bytes 33801516 | solution.py:266
  594.3 20.9 %reduce-scatter.25.cloned.1.call-done = bf16[128,1792]{1,0:T(8,128)(2,1)} async-done(((bf16[1024,1792]{1,0:T(8,128)(2,1)}), bf16[128,1792]{1,0:T(8,128)(2,1)}) %reduce-scatter.25.cloned.1.call-update) | async-done | bytes 458768 | tf_op jit(solution)/shard_map/while/body/eval_jaxpr/reduce_scatter | solution.py:284
  624.8 32.6 %all_gather.78 = bf16[224,1792]{0,1:T(8,128)(2,1)S(1)} all-gather(bf16[224,448]{0,1:T(8,128)(2,1)S(1)} %get-tuple-element.1505), channel_id=1, replica_groups=mesh['row'=4,'col'=8] {'row'}, dimensions={1}, use_global_device_ids=true | all-gather | bytes 1003520 | tf_op jit(solution)/shard_map/while/body/eval_jaxpr/all_gather | solution.py:110
  678.5 31.5 %all-gather.18.cloned.1.call-done = bf16[1,1,1024,1792]{3,2,1,0:T(8,128)(2,1)} async-done(((bf16[1,1,128,1792]{3,2,1,0:T(8,128)(2,1)}), bf16[1,1,1024,1792]{3,2,1,0:T(8,128)(2,1)}) %all-gather.18.cloned.1.call-update) | async-done | bytes 3670032 | tf_op jit(solution)/shard_map/while/body/eval_jaxpr/all_gather | solution.py:127
  736.7 48.8 %reduce-scatter.21.cloned.1.call-done = bf16[128,1792]{1,0:T(8,128)(2,1)} async-done(((bf16[1024,1792]{1,0:T(8,128)(2,1)}), bf16[128,1792]{1,0:T(8,128)(2,1)}) %reduce-scatter.21.cloned.1.call-update) | async-done | bytes 458768 | tf_op jit(solution)/shard_map/while/body/eval_jaxpr/reduce_scatter | solution.py:177
  790.0 32.4 %all-gather.22.cloned.1.call-done = bf16[1024,1792]{1,0:T(8,128)(2,1)} async-done(((bf16[128,1792]{1,0:T(8,128)(2,1)}), bf16[1024,1792]{1,0:T(8,128)(2,1)}) %all-gather.22.cloned.1.call-update) | async-done | bytes 3670032 | tf_op jit(solution)/shard_map/while/body/eval_jaxpr/all_gather | solution.py:181
  825.2 82.7 %all-gather.20.cloned.1.call-done = bf16[2,608,1792]{2,1,0:T(8,128)(2,1)} async-done(((bf16[2,152,1792]{2,1,0:T(8,128)(2,1)}), bf16[2,608,1792]{2,1,0:T(8,128)(2,1)}) %all-gather.20.cloned.1.call-update) | async-done | bytes 4358160 | tf_op jit(solution)/shard_map/while/body/eval_jaxpr/all_gather | solution.py:111
  918.3 37.6 %all-gather.24.cloned.1.call-done = bf16[608,1792]{1,0:T(8,128)(2,1)} async-done(((bf16[152,1792]{1,0:T(8,128)(2,1)}), bf16[608,1792]{1,0:T(8,128)(2,1)}) %all-gather.24.cloned.1.call-update) | async-done | bytes 2179088 | tf_op jit(solution)/shard_map/while/body/eval_jaxpr/all_gather | solution.py:112
  955.9 35.7 %all-gather.26.cloned.1.call-done = bf16[1,1,1024,1792]{3,2,1,0:T(8,128)(2,1)} async-done(((bf16[1,1,128,1792]{3,2,1,0:T(8,128)(2,1)}), bf16[1,1,1024,1792]{3,2,1,0:T(8,128)(2,1)}) %all-gather.26.cloned.1.call-update) | async-done | bytes 3670032 | tf_op jit(solution)/shard_map/while/body/eval_jaxpr/all_gather | solution.py:199
  1007.2 48.9 %reduce-scatter.23.cloned.1.call-done = bf16[128,1792]{1,0:T(8,128)(2,1)} async-done(((bf16[1024,1792]{1,0:T(8,128)(2,1)}), bf16[128,1792]{1,0:T(8,128)(2,1)}) %reduce-scatter.23.cloned.1.call-update) | async-done | bytes 458768 | tf_op jit(solution)/shard_map/while/body/eval_jaxpr/reduce_scatter | solution.py:212
  1069.7 25.3 %all-gather.28.cloned.1.call-done = bf16[1024,1792]{1,0:T(8,128)(2,1)} async-done(((bf16[128,1792]{1,0:T(8,128)(2,1)}), bf16[1024,1792]{1,0:T(8,128)(2,1)}) %all-gather.28.cloned.1.call-update) | async-done | bytes 3670032 | tf_op jit(solution)/shard_map/while/body/eval_jaxpr/all_gather | solution.py:219
  1099.2 55.9 %while.95 = (s32[]{:T(128)}, f32[1024,2,16]{0,2,1:T(8,128)S(1)}, f32[1024,2,112]{0,2,1:T(8,128)}, bf16[2,512,2,16]{1,0,3,2:T(2,128)(2,1)S(1)}, s32[2]{0:T(128)S(...) while((s32[]{:T(128)}, f32[1024,2,16]{0,2,1:T(8,128)S(1)}, ...), condition=%wide.region_12.12_spmd.clone, body=%wide.region_10.11_spmd.clone.sunk | while | flops 1317081600 | bytes 33801516 | solution.py:266
  1257.4 42.2 %psum.7 = f32[2,1792]{1,0:T(2,128)S(1)} all-reduce(f32[2,1792]{1,0:T(2,128)S(1)} %copy-done.56), channel_id=1, replica_groups=mesh['row'=4,'col'=8] {'row','col'}, use_global_device_ids=true, to_apply=%region_23.24 | all-reduce | flops 3584 | bytes 28672 | tf_op jit(solution)/shard_map/psum | solution.py:338
  1347.7 77.1 %reduce-scatter.19.cloned.1.call-done = bf16[152,3584]{1,0:T(8,128)(2,1)} async-done(((bf16[608,3584]{1,0:T(8,128)(2,1)}), bf16[152,3584]{1,0:T(8,128)(2,1)}) %reduce-scatter.19.cloned.1.call-update) | async-done | bytes 1089552
  (623 shorter events, 533.1 us)
Async XLA Ops:
  18.3 92.3 %all-gather.18.cloned.1.call-start = ((), (), s32[]{:S(2)}) async-start(), calls=%async_computation.13 | async-start | bytes 4128768 | tf_op jit(solution)/shard_map/while/body/eval_jaxpr/all_gather | solution.py:127
  19.2 166.9 %reduce-scatter.21.cloned.1.call-start = ((), (), s32[]{:S(2)}) async-start(), calls=%async_computation.15 | async-start | bytes 4128768 | tf_op jit(solution)/shard_map/while/body/eval_jaxpr/reduce_scatter | solution.py:177
  137.2 85.7 %all-gather.22.cloned.1.call-start = ((), (), s32[]{:S(2)}) async-start(), calls=%async_computation.16 | async-start | bytes 4128768 | tf_op jit(solution)/shard_map/while/body/eval_jaxpr/all_gather | solution.py:181
  188.0 120.4 %all-gather.20.cloned.1.call-start = ((), (), s32[]{:S(2)}) async-start(), calls=%async_computation.14 | async-start | bytes 5447680 | tf_op jit(solution)/shard_map/while/body/eval_jaxpr/all_gather | solution.py:111
  188.6 167.8 %all-gather.24.cloned.1.call-start = ((), (), s32[]{:S(2)}) async-start(), calls=%async_computation.17 | async-start | bytes 2723840 | tf_op jit(solution)/shard_map/while/body/eval_jaxpr/all_gather | solution.py:112
  189.2 203.1 %all-gather.26.cloned.1.call-start = ((), (), s32[]{:S(2)}) async-start(), calls=%async_computation.18 | async-start | bytes 4128768 | tf_op jit(solution)/shard_map/while/body/eval_jaxpr/all_gather | solution.py:199
  190.1 266.6 %reduce-scatter.23.cloned.1.call-start = ((), (), s32[]{:S(2)}) async-start(), calls=%async_computation.19 | async-start | bytes 4128768 | tf_op jit(solution)/shard_map/while/body/eval_jaxpr/reduce_scatter | solution.py:212
  407.8 87.9 %all-gather.28.cloned.1.call-start = ((), (), s32[]{:S(2)}) async-start(), calls=%async_computation.20 | async-start | bytes 4128768 | tf_op jit(solution)/shard_map/while/body/eval_jaxpr/all_gather | solution.py:219
  461.0 122.7 %reduce-scatter.27.cloned.1.call-start = ((), (), s32[]{:S(2)}) async-start(), calls=%async_computation.22 | async-start | bytes 4128768 | tf_op jit(solution)/shard_map/while/body/eval_jaxpr/reduce_scatter | solution.py:195
  470.2 145.1 %reduce-scatter.25.cloned.1.call-start = ((), (), s32[]{:S(2)}) async-start(), calls=%async_computation.21 | async-start | bytes 4128768 | tf_op jit(solution)/shard_map/while/body/eval_jaxpr/reduce_scatter | solution.py:284
  620.4 89.6 %all-gather.18.cloned.1.call-start = ((), (), s32[]{:S(2)}) async-start(), calls=%async_computation.13 | async-start | bytes 4128768 | tf_op jit(solution)/shard_map/while/body/eval_jaxpr/all_gather | solution.py:127
  621.3 164.2 %reduce-scatter.21.cloned.1.call-start = ((), (), s32[]{:S(2)}) async-start(), calls=%async_computation.15 | async-start | bytes 4128768 | tf_op jit(solution)/shard_map/while/body/eval_jaxpr/reduce_scatter | solution.py:177
  736.6 85.7 %all-gather.22.cloned.1.call-start = ((), (), s32[]{:S(2)}) async-start(), calls=%async_computation.16 | async-start | bytes 4128768 | tf_op jit(solution)/shard_map/while/body/eval_jaxpr/all_gather | solution.py:181
  787.5 120.4 %all-gather.20.cloned.1.call-start = ((), (), s32[]{:S(2)}) async-start(), calls=%async_computation.14 | async-start | bytes 5447680 | tf_op jit(solution)/shard_map/while/body/eval_jaxpr/all_gather | solution.py:111
  788.1 167.8 %all-gather.24.cloned.1.call-start = ((), (), s32[]{:S(2)}) async-start(), calls=%async_computation.17 | async-start | bytes 2723840 | tf_op jit(solution)/shard_map/while/body/eval_jaxpr/all_gather | solution.py:112
  788.6 202.9 %all-gather.26.cloned.1.call-start = ((), (), s32[]{:S(2)}) async-start(), calls=%async_computation.18 | async-start | bytes 4128768 | tf_op jit(solution)/shard_map/while/body/eval_jaxpr/all_gather | solution.py:199
  789.5 266.5 %reduce-scatter.23.cloned.1.call-start = ((), (), s32[]{:S(2)}) async-start(), calls=%async_computation.19 | async-start | bytes 4128768 | tf_op jit(solution)/shard_map/while/body/eval_jaxpr/reduce_scatter | solution.py:212
  1007.1 87.9 %all-gather.28.cloned.1.call-start = ((), (), s32[]{:S(2)}) async-start(), calls=%async_computation.20 | async-start | bytes 4128768 | tf_op jit(solution)/shard_map/while/body/eval_jaxpr/all_gather | solution.py:219
  1060.4 126.9 %reduce-scatter.27.cloned.1.call-start = ((), (), s32[]{:S(2)}) async-start(), calls=%async_computation.22 | async-start | bytes 4128768 | tf_op jit(solution)/shard_map/while/body/eval_jaxpr/reduce_scatter | solution.py:195
  1069.5 144.8 %reduce-scatter.25.cloned.1.call-start = ((), (), s32[]{:S(2)}) async-start(), calls=%async_computation.21 | async-start | bytes 4128768 | tf_op jit(solution)/shard_map/while/body/eval_jaxpr/reduce_scatter | solution.py:284
  1225.9 86.8 %reduce-scatter.17.cloned.1.call-start = ((), (), s32[]{:S(2)}) async-start(), calls=%async_computation.10 | async-start | bytes 1146880
  1228.7 87.4 %reduce-scatter.13.cloned.1.call-start = ((), (), s32[]{:S(2)}) async-start(), calls=%async_computation.8 | async-start | bytes 2293760 | tf_op jit(solution)/shard_map/reduce_scatter | solution.py:319
  1232.3 110.9 %reduce-scatter.15.cloned.1.call-start = ((), (), s32[]{:S(2)}) async-start(), calls=%async_computation.9 | async-start | bytes 2723840 | tf_op jit(solution)/shard_map/reduce_scatter | solution.py:331
  1236.2 188.7 %reduce-scatter.19.cloned.1.call-start = ((), (), s32[]{:S(2)}) async-start(), calls=%async_computation.11 | async-start | bytes 5447680
  (164 other events, 3777.0 us)
Sparse Core Ops, SparseCore 0:
  20.6 53.2 all-gather.15
  76.5 33.9 all-gather.17
  137.3 48.6 reduce-scatter.20
  188.4 34.4 all-gather.21
  224.9 83.4 all-gather.19
  310.4 46.0 all-gather.23
  358.9 33.3 all-gather.25
  407.9 48.7 reduce-scatter.22
  461.2 34.4 all-gather.27
  499.4 48.7 reduce-scatter.26
  566.4 48.7 reduce-scatter.24
  622.6 52.0 all-gather.15
  677.3 32.6 all-gather.17
  736.7 48.7 reduce-scatter.20
  787.8 34.4 all-gather.21
  824.3 83.4 all-gather.19
  909.8 46.0 all-gather.23
  958.2 33.3 all-gather.25
  1007.2 48.7 reduce-scatter.22
  1060.5 34.4 all-gather.27
  1098.9 48.6 reduce-scatter.26
  1165.6 48.6 reduce-scatter.24
Sparse Core Ops, SparseCore 1:
  1229.2 25.1 reduce-scatter.16
  1257.1 39.2 reduce-scatter.12
  1299.1 44.0 reduce-scatter.14
  1345.6 79.2 reduce-scatter.18
where the time goes:
time: 1450 us; the launch traced here: 1440 us
  waiting for transfers between devices  858 us (59%)
  matrix products  244 us (17%)
  blocking collectives  119 us (8%)
  other arithmetic  103 us (7%)
  local copies, waits for them, and re-layouts  76.9 us (5%)
  loops' own time  24 us (2%)
  between operations  16.2 us (1%)
    all_gather x2, waiting for transfers between devices, fetch_weights(): lax.all_gather(up_weight.astype(jnp.bfloat16), 'row', axis=1, tiled=True)  165 us
    reduce_scatter x2, waiting for transfers between devices, micro_step(): lax.psum_scatter(back_two.astype(jnp.bfloat16), 'col', scatter_dimension=...  97.7 us
    reduce_scatter x2, waiting for transfers between devices, micro_step(): lax.psum_scatter(partial_mix.astype(jnp.bfloat16), 'col', scatter_dimensi...  97.7 us
    unnamed x6, waiting for transfers between devices  77.2 us
    all_gather x2, waiting for transfers between devices, fetch_weights(): lax.all_gather(down_weight.astype(jnp.bfloat16), 'row', axis=0, tiled=True)  75.2 us
    all_gather x2, waiting for transfers between devices, micro_step(): cot_full = lax.all_gather(cot_part, 'col', axis=0, tiled=True)  71.5 us
    all_gather x2, blocking collectives, fetch_weights(): lax.all_gather(out_weight.astype(jnp.bfloat16), 'row', axis=1, tiled=True)  65.5 us
    all_gather x2, waiting for transfers between devices, micro_step(): lax.all_gather(resid_col.astype(jnp.bfloat16), 'col', axis=0, tiled=True)  65 us
  transfers between devices with their start and end apart: 26, of which 22 were waited for; matrix products, arithmetic and copies ran while one was open for 20% of the time, Pallas kernels for 0%

commit v1 on v0

v1 whole, which is shorter than its diff:
```python
import functools
import math

import jax
import jax.numpy as jnp
from jax import lax
from jax.experimental import pallas as pl
from jax.experimental.pallas import tpu as pltpu
from jax.sharding import PartitionSpec as P

D = 1792
FF = 4864
STEP = 10


NORM_EPSILON = 1e-05
BETA_ONE = 0.9
BETA_TWO = 0.95
ADAM_EPSILON = 1e-08
DECAY_RATE = 0.1
VECTOR_RATE = 0.5

LANES = 128
BLOCK_T = 256


def silu_grad(tensor):
    sigmoid_val = jax.nn.sigmoid(tensor)
    return sigmoid_val * (1.0 + tensor * (1.0 - sigmoid_val))


def low(tensor):
    return tensor.astype(jnp.bfloat16)


def wide(tensor):
    return tensor.astype(jnp.float32)


def dot_nn(left_side, right_side):
    return lax.dot_general(
        left_side, right_side, (((1,), (0,)), ((), ())), preferred_element_type=jnp.float32
    )


def dot_tn(left_side, right_side):
    return lax.dot_general(
        left_side, right_side, (((0,), (0,)), ((), ())), preferred_element_type=jnp.float32
    )


def dot_nt(left_side, right_side):
    return lax.dot_general(
        left_side, right_side, (((1,), (1,)), ((), ())), preferred_element_type=jnp.float32
    )


def row_scale(tensor):
    return lax.rsqrt(jnp.mean(tensor * tensor, axis=1, keepdims=True) + NORM_EPSILON)


def adam_update(weight, gradient, moment_one, moment_two, step_rate, decay_rate):
    first_new = BETA_ONE * moment_one + (1.0 - BETA_ONE) * gradient
    second_new = BETA_TWO * moment_two + (1.0 - BETA_TWO) * gradient * gradient
    first_hat = first_new / (1.0 - BETA_ONE**STEP)
    second_hat = second_new / (1.0 - BETA_TWO**STEP)
    weight_new = weight - step_rate * (
        first_hat / (jnp.sqrt(second_hat) + ADAM_EPSILON) + decay_rate * weight
    )
    return (first_new, second_new, weight_new)


def col_masks(col_count, core):
    bits = [1 << place for place in range(1, col_count.bit_length() - 1)]
    return bits if core == 0 else bits[::-1]


def chip_perm(col_count, step):
    return [(i, i ^ col_masks(col_count, i & 1)[step]) for i in range(col_count)]


def core_perm(col_count):
    return [(i, i ^ 1) for i in range(col_count)]


def col_steps(col_count):
    return col_count.bit_length() - 2


def slots_of_chunks(col_count):
    table = []
    for me in range(col_count):
        row = [0] * col_count
        for half in range(2):
            origin = me ^ half
            masks = col_masks(col_count, origin & 1)
            for slot in range(col_count // 2):
                chunk = origin
                for step, mask in enumerate(masks):
                    if slot >> step & 1:
                        chunk ^= mask
                row[chunk] = half * (col_count // 2) + slot
        table.append(row)
    return jnp.asarray(table, jnp.int32)[lax.axis_index("col")]


class Line:
    def __init__(self):
        self.marks = ()

    def hold(self, *arrays):
        return lax.optimization_barrier(arrays + self.marks)[: len(arrays)]

    def mark(self, *arrays):
        self.marks = arrays


class Stage:
    def __init__(self, steps):
        self.steps, self.ended, self.result = steps, False, None
        self.advance()

    def advance(self):
        if not self.ended:
            try:
                next(self.steps)
            except StopIteration as stop:
                self.ended, self.result = True, stop.value


def advance(*stages):
    for stage in stages:
        stage.advance()


def finish(stage):
    while not stage.ended:
        stage.advance()
    return stage.result


def gather_col(line, part, col_count):
    (held,) = line.hold(part)
    line.mark(held)
    arrived = lax.ppermute(held, "col", chip_perm(col_count, 0))
    for step in range(1, col_steps(col_count)):
        yield
        (arrived,) = line.hold(arrived)
        held = jnp.concatenate([held, arrived], axis=0)
        line.mark(held)
        arrived = lax.ppermute(held, "col", chip_perm(col_count, step))
    other_held = lax.ppermute(held, "col", core_perm(col_count))
    yield
    (arrived,) = line.hold(arrived)
    line.mark(arrived)
    other_arrived = lax.ppermute(arrived, "col", core_perm(col_count))
    yield
    other_held, other_arrived = line.hold(other_held, other_arrived)
    line.mark(other_held, other_arrived)
    return [held, arrived, other_held, other_arrived]


def scatter_col(line, own, other, col_count):
    line.mark(own, other)
    arrived = lax.ppermute(other, "col", core_perm(col_count))
    last_step = col_steps(col_count) - 1
    yield
    (arrived,) = line.hold(arrived)
    upper = low(wide(own[1]) + wide(arrived[1]))
    line.mark(upper)
    lower = arrived[0]
    arrived = lax.ppermute(upper, "col", chip_perm(col_count, last_step))
    yield
    arrived, lower = line.hold(arrived, lower)
    total = wide(own[0]) + wide(lower) + wide(arrived)
    for step in reversed(range(last_step)):
        rows = total.shape[0] // 2
        send = low(total[rows:])
        line.mark(send)
        arrived = lax.ppermute(send, "col", chip_perm(col_count, step))
        yield
        (arrived,) = line.hold(arrived)
        total = wide(total[:rows]) + wide(arrived)
    return total


def sum_over(tensor, axis, count):
    bit = 1
    while bit < count:
        tensor = tensor + lax.ppermute(tensor, axis, [(i, i ^ bit) for i in range(count)])
        bit *= 2
    return tensor


def head_parts(feat_dim, head_dim, inv_ref, proj_ref, taps_ref, link_ref, p_ref):
    length = p_ref.shape[0]
    chunks = inv_ref.shape[0]
    rows = length // chunks
    for chunk in range(chunks):
        source = pl.multiple_of(inv_ref[chunk] * rows, rows)
        p_ref[chunk * rows : (chunk + 1) * rows, :] = proj_ref[pl.ds(source, rows), :]
    packed = p_ref[...]
    pack_dim = packed.shape[1]
    lane = lax.broadcasted_iota(jnp.int32, (length, LANES), 1)
    first = packed[:, :LANES]
    queries = low(jnp.where(lane < feat_dim, first, 0.0))
    keys = low(jnp.where(lane < feat_dim, pltpu.roll(first, LANES - feat_dim, 1), 0.0))
    inner = pltpu.roll(packed, pack_dim - 2 * feat_dim, 1)[:, :LANES]
    inner = jnp.where(lane < head_dim, inner, 0.0)
    gate = pltpu.roll(packed, pack_dim - 2 * feat_dim - head_dim, 1)[:, :LANES]
    gate = jnp.where(lane < head_dim, gate, 0.0)
    taps = taps_ref[0]
    shifted = [inner]
    conv = taps[0:1, :] * inner
    for offset in range(1, taps.shape[0]):
        moved = pltpu.roll(inner, offset, 0)
        shifted.append(moved)
        conv = conv + taps[offset : offset + 1, :] * (moved * link_ref[:, offset : offset + 1])
    return queries, keys, gate, taps, shifted, conv


def kept_scores(feat_dim, block, keys, queries, segc_ref, segr_ref):
    first, last = block * BLOCK_T, (block + 1) * BLOCK_T
    score = dot_nt(keys[:last], queries[first:last]) * (1.0 / math.sqrt(feat_dim))
    key_at = lax.broadcasted_iota(jnp.int32, (last, BLOCK_T), 0)
    query_at = first + lax.broadcasted_iota(jnp.int32, (last, BLOCK_T), 1)
    kept = (key_at <= query_at) & (segc_ref[:last, :] == segr_ref[:, first:last])
    kern = jnp.where(kept, 1.0 + score + 0.5 * score * score, 0.0)
    scale = 1.0 / jnp.sum(kern, axis=0, keepdims=True)
    return score, kept, kern * scale, scale


def forward_kernel(
    feat_dim, head_dim, inv_ref, proj_ref, taps_ref, link_ref, segc_ref, segr_ref, out_ref, p_ref
):
    queries, keys, gate, taps, shifted, conv = head_parts(
        feat_dim, head_dim, inv_ref, proj_ref, taps_ref, link_ref, p_ref
    )
    length = p_ref.shape[0]
    values = low(conv * (gate * jax.nn.sigmoid(gate))).T
    blocks = []
    for block in range(length // BLOCK_T):
        score, kept, probs, scale = kept_scores(
            feat_dim, block, keys, queries, segc_ref, segr_ref
        )
        last = (block + 1) * BLOCK_T
        blocks.append(low(dot_nn(values[:, :last], low(probs)).T))
    attended = jnp.concatenate(blocks, axis=0)
    chunks = inv_ref.shape[0]
    rows = length // chunks
    for chunk in range(chunks):
        target = pl.multiple_of(inv_ref[chunk] * rows, rows)
        out_ref[pl.ds(target, rows), :] = attended[chunk * rows : (chunk + 1) * rows]


def backward_kernel(
    feat_dim,
    head_dim,
    inv_ref,
    proj_ref,
    grad_ref,
    taps_ref,
    link_ref,
    segc_ref,
    segr_ref,
    out_ref,
    tap_ref,
    p_ref,
    g_ref,
    dk_ref,
    dv_ref,
):
    queries, keys, gate, taps, shifted, conv = head_parts(
        feat_dim, head_dim, inv_ref, proj_ref, taps_ref, link_ref, p_ref
    )
    length = p_ref.shape[0]
    chunks = inv_ref.shape[0]
    rows = length // chunks
    for chunk in range(chunks):
        source = pl.multiple_of(inv_ref[chunk] * rows, rows)
        g_ref[chunk * rows : (chunk + 1) * rows, :] = grad_ref[pl.ds(source, rows), :]
    grad = g_ref[...]
    sigmoid_val = jax.nn.sigmoid(gate)
    gate_act = gate * sigmoid_val
    values = low(conv * gate_act)
    keys_turned = keys.T
    root = 1.0 / math.sqrt(feat_dim)
    dk_ref[...] = jnp.zeros_like(dk_ref)
    dv_ref[...] = jnp.zeros_like(dv_ref)
    query_grads = []
    for block in range(length // BLOCK_T):
        first, last = block * BLOCK_T, (block + 1) * BLOCK_T
        score, kept, probs, scale = kept_scores(
            feat_dim, block, keys, queries, segc_ref, segr_ref
        )
        weight_grad = dot_nt(values[:last], grad[first:last])
        row_dot = jnp.sum(weight_grad * probs, axis=0, keepdims=True)
        score_grad = low(
            jnp.where(kept, (weight_grad - row_dot) * scale * (1.0 + score), 0.0)
        )
        query_grads.append(dot_nn(keys_turned[:, :last], score_grad).T)
        dk_ref[:last, :] += dot_nn(score_grad, queries[first:last])
        dv_ref[:last, :] += dot_nn(low(probs), grad[first:last])
    grad_queries = jnp.concatenate(query_grads, axis=0) * root
    grad_keys = dk_ref[...] * root
    grad_values = dv_ref[...]
    grad_conv = grad_values * gate_act
    grad_gate = grad_values * conv * (sigmoid_val * (1.0 + gate * (1.0 - sigmoid_val)))
    grad_inner = taps[0:1, :] * grad_conv
    tap_rows = [jnp.sum(grad_conv * shifted[0], axis=0, keepdims=True)]
    for offset in range(1, taps.shape[0]):
        masked = grad_conv * link_ref[:, offset : offset + 1]
        tap_rows.append(jnp.sum(masked * shifted[offset], axis=0, keepdims=True))
        grad_inner = grad_inner + taps[offset : offset + 1, :] * pltpu.roll(
            masked, length - offset, 0
        )
    for offset, tap_row in enumerate(tap_rows):
        tap_ref[0, offset : offset + 1, :] = tap_row
    empty = jnp.zeros((length, LANES), jnp.float32)
    packed = jnp.concatenate([grad_queries + pltpu.roll(grad_keys, feat_dim, 1), empty], axis=1)
    packed = packed + pltpu.roll(jnp.concatenate([grad_inner, empty], axis=1), 2 * feat_dim, 1)
    packed = low(
        packed
        + pltpu.roll(jnp.concatenate([grad_gate, empty], axis=1), 2 * feat_dim + head_dim, 1)
    )
    for chunk in range(chunks):
        target = pl.multiple_of(inv_ref[chunk] * rows, rows)
        out_ref[pl.ds(target, rows), :] = packed[chunk * rows : (chunk + 1) * rows]


def whole_spec(shape):
    return pl.BlockSpec(shape, lambda head, inv: (0,) * len(shape))


def attend(inv, projected, taps, links, segc, segr, feat_dim, head_dim):
    length = projected.shape[0]
    heads, tap_count = taps.shape[0], taps.shape[1]
    pack_dim = projected.shape[1] // heads
    return pl.pallas_call(
        functools.partial(forward_kernel, feat_dim, head_dim),
        out_shape=jax.ShapeDtypeStruct((length, heads * LANES), jnp.bfloat16),
        grid_spec=pltpu.PrefetchScalarGridSpec(
            num_scalar_prefetch=1,
            grid=(heads,),
            in_specs=[
                pl.BlockSpec((length, pack_dim), lambda head, inv: (0, head)),
                pl.BlockSpec((1, tap_count, LANES), lambda head, inv: (head, 0, 0)),
                whole_spec(links.shape),
                whole_spec(segc.shape),
                whole_spec(segr.shape),
            ],
            out_specs=pl.BlockSpec((length, LANES), lambda head, inv: (0, head)),
            scratch_shapes=[pltpu.VMEM((length, pack_dim), jnp.float32)],
        ),
        compiler_params=pltpu.CompilerParams(vmem_limit_bytes=40 * 1024 * 1024),
        cost_estimate=pl.CostEstimate(
            flops=heads * length * length * LANES * 3,
            bytes_accessed=heads * length * (pack_dim * 4 + LANES * 2),
            transcendentals=heads * length * LANES,
        ),
    )(inv, projected, taps, links, segc, segr)


def attend_back(inv, projected, grad, taps, links, segc, segr, feat_dim, head_dim):
    length = projected.shape[0]
    heads, tap_count = taps.shape[0], taps.shape[1]
    pack_dim = projected.shape[1] // heads
    return pl.pallas_call(
        functools.partial(backward_kernel, feat_dim, head_dim),
        out_shape=(
            jax.ShapeDtypeStruct((length, heads * pack_dim), jnp.bfloat16),
            jax.ShapeDtypeStruct((heads, tap_count, LANES), jnp.float32),
        ),
        grid_spec=pltpu.PrefetchScalarGridSpec(
            num_scalar_prefetch=1,
            grid=(heads,),
            in_specs=[
                pl.BlockSpec((length, pack_dim), lambda head, inv: (0, head)),
                pl.BlockSpec((length, LANES), lambda head, inv: (0, head)),
                pl.BlockSpec((1, tap_count, LANES), lambda head, inv: (head, 0, 0)),
                whole_spec(links.shape),
                whole_spec(segc.shape),
                whole_spec(segr.shape),
            ],
            out_specs=(
                pl.BlockSpec((length, pack_dim), lambda head, inv: (0, head)),
                pl.BlockSpec((1, tap_count, LANES), lambda head, inv: (head, 0, 0)),
            ),
            scratch_shapes=[
                pltpu.VMEM((length, pack_dim), jnp.float32),
                pltpu.VMEM((length, LANES), jnp.bfloat16),
                pltpu.VMEM((length, LANES), jnp.float32),
                pltpu.VMEM((length, LANES), jnp.float32),
            ],
        ),
        compiler_params=pltpu.CompilerParams(vmem_limit_bytes=48 * 1024 * 1024),
        cost_estimate=pl.CostEstimate(
            flops=heads * length * length * LANES * 6,
            bytes_accessed=heads * length * (pack_dim * 6 + LANES * 2),
            transcendentals=heads * length * LANES,
        ),
    )(inv, projected, grad, taps, links, segc, segr)


def ffn_kernel(*refs):
    normed_refs, cot_refs = refs[:4], refs[4:8]
    weight_ref, turned_ref, own_ref, other_ref = refs[8:]
    hidden, width = weight_ref.shape[1:]
    rows = normed_refs[0].shape[0]
    normed = jnp.concatenate([ref[...] for ref in normed_refs], axis=0)
    cot = jnp.concatenate([ref[...] for ref in cot_refs], axis=0)
    gate = dot_nt(weight_ref[0], normed)
    up = dot_nt(weight_ref[1], normed)
    grad_hidden = dot_nt(weight_ref[2], cot)
    sigmoid_val = jax.nn.sigmoid(gate)
    gate_sig = gate * sigmoid_val
    turned_ref[0] = low(grad_hidden * up * (sigmoid_val * (1.0 + gate * (1.0 - sigmoid_val))))
    turned_ref[1] = low(grad_hidden * gate_sig)
    turned_ref[2] = low(gate_sig * up)
    back = low(
        dot_tn(
            turned_ref[:2].reshape(2 * hidden, 4 * rows), weight_ref[:2].reshape(2 * hidden, width)
        )
    )
    for block, ref in enumerate((own_ref, own_ref, other_ref, other_ref)):
        ref[block % 2] = back[block * rows : (block + 1) * rows]


def ffn_call(normed, cot, weights):
    block_rows, width = normed[0].shape
    _, hidden, _ = weights.shape
    rows = block_rows // 2
    block = pl.BlockSpec((rows, width), lambda step: (step, 0))
    half = pl.BlockSpec((2, rows, width), lambda step: (0, step, 0))
    return pl.pallas_call(
        ffn_kernel,
        grid=(block_rows // rows,),
        in_specs=[block] * 8
        + [
            pl.BlockSpec(
                weights.shape, lambda step: (0, 0, 0), pipeline_mode=pl.Buffered(buffer_count=1)
            )
        ],
        out_specs=(
            pl.BlockSpec((3, hidden, 4 * rows), lambda step: (0, 0, step)),
            half,
            half,
        ),
        out_shape=(
            jax.ShapeDtypeStruct((3, hidden, 4 * block_rows), jnp.bfloat16),
            jax.ShapeDtypeStruct((2, block_rows, width), jnp.bfloat16),
            jax.ShapeDtypeStruct((2, block_rows, width), jnp.bfloat16),
        ),
        compiler_params=pltpu.CompilerParams(vmem_limit_bytes=52 * 1024 * 1024),
        cost_estimate=pl.CostEstimate(
            flops=2 * 5 * 4 * block_rows * hidden * width,
            bytes_accessed=2 * (3 * hidden * width + 12 * block_rows * width),
            transcendentals=4 * block_rows * hidden,
        ),
    )(*normed, *cot, weights)


def ffn_sum_kernel(hidden_ref, weight_ref, own_ref, other_ref):
    rows = own_ref.shape[1]
    total = low(dot_tn(hidden_ref[0], weight_ref[0]))
    for block, ref in enumerate((own_ref, own_ref, other_ref, other_ref)):
        ref[block % 2] = total[block * rows : (block + 1) * rows]


def ffn_sum_call(turned, weights):
    _, hidden, tokens = turned.shape
    width = weights.shape[2]
    rows = tokens // 8
    half = pl.BlockSpec((2, rows, width), lambda step: (0, step, 0))
    shape = jax.ShapeDtypeStruct((2, tokens // 4, width), jnp.bfloat16)
    return pl.pallas_call(
        ffn_sum_kernel,
        grid=(2,),
        in_specs=[
            pl.BlockSpec((1, hidden, 4 * rows), lambda step: (2, 0, step)),
            pl.BlockSpec((1, hidden, width), lambda step: (2, 0, 0)),
        ],
        out_specs=(half, half),
        out_shape=(shape, shape),
        compiler_params=pltpu.CompilerParams(vmem_limit_bytes=40 * 1024 * 1024),
        cost_estimate=pl.CostEstimate(
            flops=2 * tokens * hidden * width,
            bytes_accessed=2 * (hidden * width + tokens * (hidden + width)),
            transcendentals=0,
        ),
    )(turned, weights)


def ffn_grad_kernel(micro_count, steps, *refs):
    turned_refs, block_refs, out_ref = refs[:micro_count], refs[micro_count:-1], refs[-1]
    owners, kinds, own, _ = out_ref.shape
    hidden = owners * own
    rows = block_refs[0].shape[0] // steps
    total = None
    for micro, turned_ref in enumerate(turned_refs):
        tokens = jnp.concatenate(
            [
                ref[step * rows : (step + 1) * rows, :]
                for step in range(steps)
                for ref in block_refs[4 * micro : 4 * micro + 4]
            ],
            axis=0,
        )
        part = dot_nn(turned_ref[...].reshape(kinds * hidden, turned_ref.shape[2]), tokens)
        total = part if total is None else total + part
    for owner in range(owners):
        for kind in range(kinds):
            first = kind * hidden + owner * own
            out_ref[owner, kind] = low(total[first : first + own])


def ffn_grad_call(turned, blocks, first, kinds, owners):
    micro_count = len(turned)
    _, hidden, tokens = turned[0].shape
    block_rows, width = blocks[0][0].shape
    lanes = 2 * LANES
    return pl.pallas_call(
        functools.partial(ffn_grad_kernel, micro_count, 2),
        grid=(width // lanes,),
        in_specs=[
            pl.BlockSpec(
                (kinds, hidden, tokens),
                lambda step: (first // kinds, 0, 0),
                pipeline_mode=pl.Buffered(buffer_count=1),
            )
        ]
        * micro_count
        + [pl.BlockSpec((block_rows, lanes), lambda step: (0, step))] * (4 * micro_count),
        out_specs=pl.BlockSpec(
            (owners, kinds, hidden // owners, lanes), lambda step: (0, 0, 0, step)
        ),
        out_shape=jax.ShapeDtypeStruct((owners, kinds, hidden // owners, width), jnp.bfloat16),
        compiler_params=pltpu.CompilerParams(vmem_limit_bytes=52 * 1024 * 1024),
        cost_estimate=pl.CostEstimate(
            flops=2 * kinds * micro_count * tokens * hidden * width,
            bytes_accessed=2 * (kinds * hidden * (width + tokens) + micro_count * tokens * width),
            transcendentals=0,
        ),
    )(*turned, *[block for group in blocks for block in group])


def local(
    layer_input,
    cotangent,
    segments,
    norm_gains,
    gain_mean,
    gain_square,
    conv_kernel,
    conv_mean,
    conv_square,
    mix_weight,
    mix_mean,
    mix_square,
    out_weight,
    out_mean,
    out_square,
    up_weight,
    up_mean,
    up_square,
    down_weight,
    down_mean,
    down_square,
):
    micro_count = layer_input.shape[0]
    length = segments.shape[2]
    width_all = layer_input.shape[3]
    block_d, heads, pack_dim = mix_weight.shape
    width_col = out_weight.shape[0]
    head_dim = width_col // heads
    feat_dim = (pack_dim - 2 * head_dim) // 2
    tap_count = conv_kernel.shape[0]
    row_count = lax.axis_size("row")
    col_count = lax.axis_size("col")
    hidden_own = down_weight.shape[0]
    hidden_col = hidden_own * row_count
    row_me = lax.axis_index("row")
    inv = slots_of_chunks(col_count)
    micros = range(micro_count)
    gain_one, gain_two = norm_gains[0], norm_gains[1]

    mix_own = low(mix_weight).reshape(block_d, heads * pack_dim)
    out_own = jnp.pad(
        low(out_weight).reshape(heads, head_dim, block_d), ((0, 0), (0, LANES - head_dim), (0, 0))
    )
    out_own = out_own.reshape(heads * LANES, block_d).T
    mix_out_own = jnp.concatenate([mix_own, out_own], axis=1)
    mix_out = lax.all_gather(mix_out_own, "row", axis=0, tiled=True)
    mix_full, out_full = mix_out[:, : heads * pack_dim], mix_out[:, heads * pack_dim :]
    ffn_own = low(jnp.concatenate([up_weight, down_weight[None]], axis=0))
    ffn_full = lax.all_gather(ffn_own, "row", axis=1, tiled=True)

    taps = jnp.pad(
        conv_kernel.reshape(tap_count, heads, head_dim).transpose(1, 0, 2),
        ((0, 0), (0, 0), (0, LANES - head_dim)),
    )

    def links_of(segs):
        columns = [jnp.ones((length,), jnp.float32)]
        for offset in range(1, tap_count):
            earlier = jnp.concatenate(
                [jnp.full((offset,), -1, jnp.int32), segs[: length - offset]]
            )
            columns.append((earlier == segs).astype(jnp.float32))
        return jnp.stack(columns, axis=1)

    inputs = [wide(layer_input[m, 0]) for m in micros]
    scale_one = [row_scale(x) for x in inputs]
    norm_one = [x * s * gain_one for x, s in zip(inputs, scale_one)]
    cot_own = [wide(cotangent[m, 0]) for m in micros]
    segs = [segments[m, 0] for m in micros]
    links = [links_of(sg) for sg in segs]
    segc = [sg[:, None] for sg in segs]
    segr = [sg[None, :] for sg in segs]
    first, second = micros[0], micros[-1]
    line = Line()

    def col_gather(part):
        return Stage(gather_col(line, part, col_count))

    def col_scatter(own, other):
        return Stage(scatter_col(line, own, other, col_count))

    def halves(product):
        half, rows = length // 2, length // 4
        own, other = low(product(0, half)), low(product(half, length))
        return own.reshape(2, rows, width_all), other.reshape(2, rows, width_all)

    def joined(blocks):
        full = jnp.concatenate(blocks, axis=0)
        line.mark(full)
        return full

    def start_attention(m):
        normed, mix = line.hold(normed_one[m], mix_full)
        proj = dot_nn(normed, mix)
        att = attend(inv, proj, taps, links[m], segc[m], segr[m], feat_dim, head_dim)
        projected[m], attended[m] = proj, att
        return col_scatter(*halves(lambda lo, hi: dot_nt(att[lo:hi], out_full)))

    def end_mixer(m, stage):
        resid[m] = inputs[m] + finish(stage)
        scale_two[m] = row_scale(resid[m])
        norm_two[m] = resid[m] * scale_two[m] * gain_two
        return col_gather(low(norm_two[m]))

    normed_one, cots, projected, attended, resid, scale_two, norm_two, normed_two = [
        [None] * micro_count for _ in range(8)
    ]

    one_a = col_gather(low(norm_one[first]))
    line.mark(*line.marks, ffn_own)
    advance(one_a)
    one_b = col_gather(low(norm_one[second]))
    advance(one_b, one_a)
    cot_a = col_gather(cotangent[first, 0])
    normed_one[first] = joined(finish(one_a))
    advance(one_b, cot_a)
    normed_one[second] = joined(finish(one_b))
    mix_a = start_attention(first)
    advance(cot_a)
    cot_b = col_gather(cotangent[second, 0])
    mix_b = start_attention(second)
    advance(mix_a, cot_b, mix_b)
    cots[first] = finish(cot_a)
    advance(mix_a, cot_b, mix_b)
    two_a = end_mixer(first, mix_a)
    two_b = end_mixer(second, mix_b)
    advance(two_a)
    cots[second] = finish(cot_b)
    advance(two_b)
    advance(two_a)
    normed_two[first] = finish(two_a)
    advance(two_b)
    (ffn_full,) = line.hold(ffn_full)
    line.mark(ffn_full)
    normed_two[second] = finish(two_b)

    turned, resid_grad, outputs = [[None] * micro_count for _ in range(3)]

    def start_back(m):
        held = line.hold(*normed_two[m], *cots[m])
        turned[m], own, other = ffn_call(held[:4], held[4:], ffn_full)
        return col_scatter(own, other)

    def start_ffn_sum(m):
        (held,) = line.hold(turned[m])
        return col_scatter(*ffn_sum_call(held, ffn_full))

    gain_two_sum = 0.0

    def end_back(m, stage):
        back = finish(stage)
        mean_two = jnp.mean(back * norm_two[m], axis=1, keepdims=True)
        resid_grad[m] = cot_own[m] + scale_two[m] * (
            gain_two * back - resid[m] * scale_two[m] * mean_two
        )
        gain = jnp.sum(back * resid[m] * scale_two[m], axis=0)
        return col_gather(low(resid_grad[m])), gain

    back_a = start_back(first)
    back_b = start_back(second)
    advance(back_a, back_b)

    def ffn_grads(blocks, kind, kinds):
        held = line.hold(*turned)
        grads = ffn_grad_call(held, blocks, kind, kinds, row_count)
        line.mark(grads)
        grads = grads.reshape(kinds * hidden_col, width_all)
        return lax.psum_scatter(grads, "row", scatter_dimension=0, tiled=True)

    red_down = ffn_grads(cots, 2, 1)
    red_up = ffn_grads(normed_two, 0, 2)
    advance(back_a)
    low_a, gain_part = end_back(first, back_a)
    gain_two_sum = gain_two_sum + gain_part
    advance(back_b, low_a)
    low_b, gain_part = end_back(second, back_b)
    gain_two_sum = gain_two_sum + gain_part
    sum_a = start_ffn_sum(first)
    advance(low_a, low_b)

    projected_grads, resid_low, grads_input = [[None] * micro_count for _ in range(3)]
    tap_parts = [None] * micro_count
    gain_one_parts = [None] * micro_count

    def start_attention_back(m, stage):
        resid_low[m] = joined(finish(stage))
        grad_att = low(dot_nn(resid_low[m], out_full))
        grad_proj, tap_parts[m] = attend_back(
            inv, projected[m], grad_att, taps, links[m], segc[m], segr[m], feat_dim, head_dim
        )
        projected_grads[m] = grad_proj
        return col_scatter(*halves(lambda lo, hi: dot_nt(grad_proj[lo:hi], mix_full)))

    def end_input(m, stage):
        back = finish(stage)
        mean_one = jnp.mean(back * norm_one[m], axis=1, keepdims=True)
        grads_input[m] = resid_grad[m] + scale_one[m] * (
            gain_one * back - inputs[m] * scale_one[m] * mean_one
        )
        gain_one_parts[m] = jnp.sum(back * inputs[m] * scale_one[m], axis=0)
        line.mark(gain_one_parts[m])

    def end_ffn_sum(m, stage):
        outputs[m] = low(resid[m] + finish(stage))
        line.mark(outputs[m])

    (red_down,) = line.hold(red_down)
    line.mark(red_down)
    input_a = start_attention_back(first, low_a)
    advance(low_b, sum_a)
    input_b = start_attention_back(second, low_b)
    grad_projs = line.hold(*projected_grads)
    grad_both = low(
        jnp.concatenate(
            [
                sum(dot_tn(normed_one[m], grad_projs[m]) for m in micros),
                sum(dot_tn(resid_low[m], attended[m]) for m in micros),
            ],
            axis=1,
        )
    )
    line.mark(grad_both)
    advance(input_a, input_b, sum_a)
    sum_b = start_ffn_sum(second)
    red_up, grad_both = line.hold(red_up, grad_both)
    line.mark(grad_both)
    red_both = lax.psum_scatter(grad_both, "row", scatter_dimension=0, tiled=True)
    end_ffn_sum(first, sum_a)
    advance(input_a, sum_b, input_b)
    end_input(first, input_a)
    end_input(second, input_b)
    end_ffn_sum(second, sum_b)
    red_both = wide(red_both)
    red_mix, red_out = red_both[:, : heads * pack_dim], red_both[:, heads * pack_dim :]
    red_up = wide(red_up).reshape(2, hidden_own, width_all)
    red_down = wide(red_down)
    gain_one_sum = sum(gain_one_parts)
    tap_sum = sum(tap_parts)
    red_out = red_out.T.reshape(heads, LANES, block_d)[:, :head_dim].reshape(out_weight.shape)
    red_mix = red_mix.reshape(mix_weight.shape)
    tap_grads = tap_sum[:, :, :head_dim].transpose(1, 0, 2).reshape(tap_count, width_col)
    red_conv = sum_over(tap_grads, "row", row_count)
    red_gains = jnp.stack([gain_one_sum, gain_two_sum], axis=0)
    red_gains = sum_over(sum_over(red_gains, "col", col_count), "row", row_count)

    gain_means, gain_squares, new_gains = adam_update(
        norm_gains, red_gains, gain_mean, gain_square, VECTOR_RATE, 0.0
    )
    conv_means, conv_squares, new_kernel = adam_update(
        conv_kernel, red_conv, conv_mean, conv_square, VECTOR_RATE, 0.0
    )
    mix_means, mix_squares, new_mix = adam_update(
        mix_weight, red_mix, mix_mean, mix_square, D ** (-0.5), DECAY_RATE
    )
    out_means, out_squares, new_out = adam_update(
        out_weight, red_out, out_mean, out_square, 8.0 * D ** (-0.5), DECAY_RATE
    )
    up_means, up_squares, new_up = adam_update(
        up_weight, red_up, up_mean, up_square, D ** (-0.5), DECAY_RATE
    )
    down_means, down_squares, new_down = adam_update(
        down_weight, red_down, down_mean, down_square, FF ** (-0.5), DECAY_RATE
    )
    return (
        jnp.stack(outputs)[:, None],
        jnp.stack(grads_input)[:, None],
        gain_means,
        gain_squares,
        new_gains,
        conv_means,
        conv_squares,
        new_kernel,
        mix_means,
        mix_squares,
        new_mix,
        low(new_mix),
        out_means,
        out_squares,
        new_out,
        low(new_out),
        up_means,
        up_squares,
        new_up,
        low(new_up),
        down_means,
        down_squares,
        new_down,
        low(new_down),
    )


def solution(mesh):
    placed = (
        P(None, "row", "col", None),
        P(None, "row", "col", None),
        P(None, "row", None),
        P(),
        P(),
        P(),
        P(None, "col"),
        P(None, "col"),
        P(None, "col"),
        P("row", "col", None),
        P("row", "col", None),
        P("row", "col", None),
        P("col", "row"),
        P("col", "row"),
        P("col", "row"),
        P(None, ("row", "col"), None),
        P(None, ("row", "col"), None),
        P(None, ("row", "col"), None),
        P(("row", "col"), None),
        P(("row", "col"), None),
        P(("row", "col"), None),
    )
    return jax.shard_map(
        local,
        mesh=mesh,
        in_specs=placed,
        out_specs=(
            P(None, "row", "col", None),
            P(None, "row", "col", None),
            P(),
            P(),
            P(),
            P(None, "col"),
            P(None, "col"),
            P(None, "col"),
            P("row", "col", None),
            P("row", "col", None),
            P("row", "col", None),
            P("row", "col", None),
            P("col", "row"),
            P("col", "row"),
            P("col", "row"),
            P("col", "row"),
            P(None, ("row", "col"), None),
            P(None, ("row", "col"), None),
            P(None, ("row", "col"), None),
            P(None, ("row", "col"), None),
            P(("row", "col"), None),
            P(("row", "col"), None),
            P(("row", "col"), None),
            P(("row", "col"), None),
        ),
        check_vma=False,
    )
```

time: 1450 us -> 501 us (0.35)
  waiting for transfers between devices: 858 us -> 170 us
  matrix products: 244 us -> 33.2 us
  blocking collectives: 119 us -> 0 us
  Pallas kernels: 0 us -> 104 us
  other arithmetic: 103 us -> 55.3 us
  starting transfers between devices: 2.07 us -> 47.1 us
  loops' own time: 24 us -> 0 us
    all_gather x14 -> x2, waiting for transfers between devices: 527 us -> 3.78 us  [the longest x1 3.78 us: local(): ffn_full = lax.all_gather(ffn_own, 'row', axis=1, tiled=True)]
    reduce_scatter x10 -> x2, waiting for transfers between devices: 250 us -> 0.01 us  [ffn_grads(): return lax.psum_scatter(grads, 'row', scatter_dimension=0, tiled=True)]
    dot_general x48 -> x16, matrix products: 244 us -> 33.2 us  [the longest x4 11.5 us: dot_tn(): lax.dot_general(left_side, right_side, (((0,), (0,)), ((), ())), preferre...]
    ppermute x0 -> x63, waiting for transfers between devices: none -> 164 us  [the longest x8 43.7 us: scatter_col(): arrived = lax.ppermute(upper, 'col', chip_perm(col_count, last_step))]
    pallas_call x0 -> x10, Pallas kernels: none -> 104 us  [the longest x2 38 us: ffn_call(): pl.pallas_call(ffn_kernel, grid=(block_rows // rows,), in_specs=[block] *...]
    unnamed x6, waiting for transfers between devices: 77.2 us -> 2.59 us
    all_gather x2 -> x0, blocking collectives: 65.5 us -> none  [fetch_weights(): lax.all_gather(out_weight.astype(jnp.bfloat16), 'row', axis=1, tiled=True)]
    ppermute x0 -> x63, starting transfers between devices: none -> 46.9 us  [the longest x8 11.9 us: gather_col(): arrived = lax.ppermute(held, 'col', chip_perm(col_count, 0))]
  transfers between devices with their start and end apart: 26 -> 68, of which waited for: 22 -> 28; matrix products, arithmetic and copies ran while one was open for 20% -> 26% of each run, Pallas kernels for 0% -> 17%
where the time goes in v1:
time: 501 us; the launch traced here: 495 us
  waiting for transfers between devices  170 us (34%)
  Pallas kernels  104 us (21%)
  local copies, waits for them, and re-layouts  69.6 us (14%)
  other arithmetic  55.3 us (11%)
  starting transfers between devices  47.1 us (9%)
  matrix products  33.2 us (7%)
  between operations  16 us (3%)
    ppermute x8, waiting for transfers between devices, scatter_col(): arrived = lax.ppermute(upper, 'col', chip_perm(col_count, last_step))  43.7 us
    unnamed x253, local copies, waits for them, and re-layouts  43.4 us
    ppermute x8, waiting for transfers between devices, gather_col(): arrived = lax.ppermute(held, 'col', chip_perm(col_count, 0))  40.4 us
    pallas_call x2, Pallas kernels, ffn_call(): pl.pallas_call(ffn_kernel, grid=(block_rows // rows,), in_specs=[block] *...  38 us
    convert_element_type x20, other arithmetic, low(): return tensor.astype(jnp.bfloat16)  33.6 us
    ppermute x8, waiting for transfers between devices, gather_col(): arrived = lax.ppermute(held, 'col', chip_perm(col_count, step))  32.9 us
    ppermute x8, waiting for transfers between devices, scatter_col(): arrived = lax.ppermute(send, 'col', chip_perm(col_count, step))  30.3 us
    pallas_call x2, Pallas kernels, ffn_grad_call(): pl.pallas_call(functools.partial(ffn_grad_kernel, micro_count, 2), grid=(...  25.4 us
  transfers between devices with their start and end apart: 68, of which 28 were waited for; matrix products, arithmetic and copies ran while one was open for 26% of the time, Pallas kernels for 17%

profile of v1, /device:TPU:0, one launch (start us, length us, event | category | flops | bytes accessed | tf_op | source)
XLA Modules:
  0.0 495.1 jit_solution(1826620592256095304)
XLA Ops:
  27.7 10.9 %collective-permute-done.2 = bf16[128,1792]{1,0:T(8,128)(2,1)S(1)} collective-permute-done((bf16[128,1792]{1,0:T(8,128)(2,1)S(1)}, bf16[128,1792]{1,0:T(8,128)(2,1)S(1)}, u32[]{:S(2)}, u32[]{:S(2)}) %collective-permute-start.2) | collective-permute-done | bytes 458784 | tf_op jit(solution)/shard_map/ppermute | solution.py:145
  44.5 16.0 %collective-permute-done.5 = bf16[256,1792]{1,0:T(8,128)(2,1)} collective-permute-done((bf16[256,1792]{1,0:T(8,128)(2,1)}, bf16[256,1792]{1,0:T(8,128)(2,1)}, u32[]{:S(2)}, u32[]{:S(2)}) %collective-permute-start.5) | collective-permute-done | bytes 917536 | tf_op jit(solution)/shard_map/ppermute | solution.py:151
  77.8 6.1 %shard_map.397 = bf16[1024,256]{1,0:T(8,128)(2,1)S(1)} custom-call(s32[8]{0:T(128)S(1)} %dynamic-slice_bitcast_fusion.inv_ref, f32[1024,512]{1,0:T(8,128)S(1)} %fusion.89.proj_ref, f32[2,3,128]{2,1,0:T(4,128)S(1)} %pad.11.taps_ref, f32[1024,3]{1,0:T(8,128)S(1)} %copy.72.link_ref, s32[1024,1]{1,0:T(8,128)S(1)} %copy.73.segc_ref, ...), custom_call_target="tpu_custom_call" | custom-call | flops 805306368 | bytes 2621440 | tf_op jit(solution)/shard_map/pallas_call | solution.py:339
  86.9 6.0 %shard_map.398 = bf16[1024,256]{1,0:T(8,128)(2,1)S(1)} custom-call(s32[8]{0:T(128)S(1)} %dynamic-slice_bitcast_fusion.inv_ref, f32[1024,512]{1,0:T(8,128)S(1)} %fusion.90.proj_ref, f32[2,3,128]{2,1,0:T(4,128)S(1)} %pad.11.taps_ref, f32[1024,3]{1,0:T(8,128)S(1)} %copy-done.4, s32[1024,1]{1,0:T(8,128)S(1)} %copy-done.6, s32[1,1024]{1,0:T(1,128)S(1)} %get-tuple-element.390.segr_ref), custom_call_target="tpu_custom_call" | custom-call | flops 805306368 | bytes 2621440 | tf_op jit(solution)/shard_map/pallas_call | solution.py:339
  96.7 6.2 %collective-permute-done.15 = bf16[128,1792]{1,0:T(8,128)(2,1)S(1)} collective-permute-done((bf16[128,1792]{1,0:T(8,128)(2,1)S(1)}, bf16[128,1792]{1,0:T(8,128)(2,1)S(1)}, u32[]{:S(2)}, u32[]{:S(2)}) %collective-permute-start.15) | collective-permute-done | bytes 458784 | tf_op jit(solution)/shard_map/ppermute | solution.py:145
  106.4 20.0 %collective-permute-done.11 = bf16[256,1792]{1,0:T(8,128)(2,1)S(1)} collective-permute-done((bf16[256,1792]{1,0:T(8,128)(2,1)S(1)}, bf16[256,1792]{1,0:T(8,128)(2,1)S(1)}, u32[]{:S(2)}, u32[]{:S(2)}) %collective-permute-start.11) | collective-permute-done | bytes 917536 | tf_op jit(solution)/shard_map/ppermute | solution.py:172
  127.4 13.7 %collective-permute-done.17 = bf16[256,1792]{1,0:T(8,128)(2,1)S(1)} collective-permute-done((bf16[256,1792]{1,0:T(8,128)(2,1)S(1)}, bf16[256,1792]{1,0:T(8,128)(2,1)S(1)}, u32[]{:S(2)}, u32[]{:S(2)}) %collective-permute-start.17) | collective-permute-done | bytes 917536 | tf_op jit(solution)/shard_map/ppermute | solution.py:172
  144.2 5.9 %collective-permute-done.20 = bf16[128,1792]{1,0:T(8,128)(2,1)S(1)} collective-permute-done((bf16[128,1792]{1,0:T(8,128)(2,1)S(1)}, bf16[128,1792]{1,0:T(8,128)(2,1)S(1)}, u32[]{:S(2)}, u32[]{:S(2)}) %collective-permute-start.20) | collective-permute-done | bytes 458784 | tf_op jit(solution)/shard_map/ppermute | solution.py:180
  157.8 11.3 %collective-permute-done.22 = bf16[128,1792]{1,0:T(8,128)(2,1)S(1)} collective-permute-done((bf16[128,1792]{1,0:T(8,128)(2,1)S(1)}, bf16[128,1792]{1,0:T(8,128)(2,1)S(1)}, u32[]{:S(2)}, u32[]{:S(2)}) %collective-permute-start.22) | collective-permute-done | bytes 458784 | tf_op jit(solution)/shard_map/ppermute | solution.py:145
  174.3 12.0 %collective-permute-done.28.refs_1_.refs_7_ = bf16[256,1792]{1,0:T(8,128)(2,1)} collective-permute-done((bf16[256,1792]{1,0:T(8,128)(2,1)}, bf16[256,1792]{1,0:T(8,128)(2,1)}, u32[]{:S(2)}, u32[]{:S(2)}) %collective-permute-start.28) | collective-permute-done | bytes 917536 | tf_op jit(solution)/shard_map/ppermute | solution.py:151
  192.6 19.0 %shard_map.399 = (bf16[3,608,1024]{2,1,0:T(8,128)(2,1)}, bf16[2,256,1792]{2,1,0:T(8,128)(2,1)}, bf16[2,256,1792]{2,1,0:T(8,128)(2,1)}) custom-call(bf16[256,1792]{1,0:T(8,128)(2,1)S(1)} %copy-done.22, bf16[256,1792]{1,0:T(8,128)(2,1)S(1)} %copy-done.26, bf16[256,1792]{1,0:T(8,128)(2,1)} %copy-done.109, bf16[256,1792]{1,0:T(8,128)(2,1)} %copy-done.110, ...), custom_call_target="tpu_custom_call" | custom-call | flops 11156848640 | bytes 17547264 | tf_op jit(solution)/shard_map/pallas_call | solution.py:435
  211.6 19.1 %shard_map.400 = (bf16[3,608,1024]{2,1,0:T(8,128)(2,1)}, bf16[2,256,1792]{2,1,0:T(8,128)(2,1)}, bf16[2,256,1792]{2,1,0:T(8,128)(2,1)}) custom-call(bf16[256,1792]{1,0:T(8,128)(2,1)} %constant_dynamic-update-slice_fusion.18.refs_0_.refs_6_, bf16[256,1792]{1,0:T(8,128)(2,1)} %collective-permute-done.28.refs_1_.refs_7_, ...), custom_call_target="tpu_custom_call" | custom-call | flops 11156848640 | bytes 17547264 | tf_op jit(solution)/shard_map/pallas_call | solution.py:435
  238.5 10.0 %shard_map.401 = bf16[4,1,152,1792]{3,2,1,0:T(8,128)(2,1)} custom-call(bf16[3,608,1024]{2,1,0:T(8,128)(2,1)} %get-tuple-element.220.refs_0_.hidden_ref, bf16[3,608,1024]{2,1,0:T(8,128)(2,1)} %get-tuple-element.240.refs_1_.hidden_ref, bf16[256,1792]{1,0:T(8,128)(2,1)S(1)} %copy-done.14, bf16[256,1792]{1,0:T(8,128)(2,1)S(1)} %copy-done.20, ...), custom_call_target="tpu_custom_call" | custom-call | flops 4462739456 | bytes 10764288 | tf_op jit(solution)/shard_map/pallas_call | solution.py:522
  251.0 15.4 %shard_map.402 = bf16[4,2,152,1792]{3,2,1,0:T(8,128)(2,1)} custom-call(bf16[3,608,1024]{2,1,0:T(8,128)(2,1)} %get-tuple-element.220.refs_0_.hidden_ref, bf16[3,608,1024]{2,1,0:T(8,128)(2,1)} %get-tuple-element.240.refs_1_.hidden_ref, bf16[256,1792]{1,0:T(8,128)(2,1)S(1)} %copy-done.23, bf16[256,1792]{1,0:T(8,128)(2,1)S(1)} %copy-done.27, ...), custom_call_target="tpu_custom_call" | custom-call | flops 8925478912 | bytes 14188544 | tf_op jit(solution)/shard_map/pallas_call | solution.py:522
  269.5 7.2 %collective-permute-done.34 = bf16[128,1792]{1,0:T(8,128)(2,1)S(1)} collective-permute-done((bf16[128,1792]{1,0:T(8,128)(2,1)S(1)}, bf16[128,1792]{1,0:T(8,128)(2,1)S(1)}, u32[]{:S(2)}, u32[]{:S(2)}) %collective-permute-start.34) | collective-permute-done | bytes 458784 | tf_op jit(solution)/shard_map/ppermute | solution.py:180
  288.2 6.7 %collective-permute-done.35 = bf16[128,1792]{1,0:T(8,128)(2,1)S(1)} collective-permute-done((bf16[128,1792]{1,0:T(8,128)(2,1)S(1)}, bf16[128,1792]{1,0:T(8,128)(2,1)S(1)}, u32[]{:S(2)}, u32[]{:S(2)}) %collective-permute-start.35) | collective-permute-done | bytes 458784 | tf_op jit(solution)/shard_map/ppermute | solution.py:180
  321.9 10.2 %shard_map.404 = (bf16[1024,512]{1,0:T(8,128)(2,1)S(1)}, f32[2,3,128]{2,1,0:T(4,128)S(1)}) custom-call(s32[8]{0:T(128)S(1)} %dynamic-slice_bitcast_fusion.inv_ref, f32[1024,512]{1,0:T(8,128)S(1)} %copy-done.3, bf16[1024,256]{1,0:T(8,128)(2,1)S(1)} %convolution_convert_fusion.9.grad_ref, f32[2,3,128]{2,1,0:T(4,128)S(1)} %pad.11.taps_ref, ...), custom_call_target="tpu_custom_call" | custom-call | flops 1610612736 | bytes 3670016 | tf_op jit(solution)/shard_map/pallas_call | solution.py:368
  354.8 10.2 %shard_map.405 = (bf16[1024,512]{1,0:T(8,128)(2,1)S(1)}, f32[2,3,128]{2,1,0:T(4,128)S(1)}) custom-call(s32[8]{0:T(128)S(1)} %dynamic-slice_bitcast_fusion.inv_ref, f32[1024,512]{1,0:T(8,128)S(1)} %fusion.90.proj_ref, bf16[1024,256]{1,0:T(8,128)(2,1)S(1)} %convolution_convert_fusion.8.grad_ref, f32[2,3,128]{2,1,0:T(4,128)S(1)} %pad.11.taps_ref, ...), custom_call_target="tpu_custom_call" | custom-call | flops 1610612736 | bytes 3670016 | tf_op jit(solution)/shard_map/pallas_call | solution.py:368
  367.6 4.7 fusion.91
  405.9 4.9 copy.86
  410.8 5.3 %collective-permute-done.48 = bf16[128,1792]{1,0:T(8,128)(2,1)} collective-permute-done((bf16[128,1792]{1,0:T(8,128)(2,1)S(1)}, bf16[128,1792]{1,0:T(8,128)(2,1)}, u32[]{:S(2)}, u32[]{:S(2)}) %collective-permute-start.48) | collective-permute-done | bytes 458784 | tf_op jit(solution)/shard_map/ppermute | solution.py:180
  426.5 7.3 %collective-permute-done.52 = bf16[256,1792]{1,0:T(8,128)(2,1)} collective-permute-done((bf16[256,1792]{1,0:T(8,128)(2,1)}, bf16[256,1792]{1,0:T(8,128)(2,1)}, u32[]{:S(2)}, u32[]{:S(2)}) %collective-permute-start.52) | collective-permute-done | bytes 917536 | tf_op jit(solution)/shard_map/ppermute | solution.py:172
  436.3 5.6 %fusion.76 = (bf16[2,152,1792]{2,1,0:T(8,128)(2,1)}, f32[2,152,1792]{2,1,0:T(8,128)}, f32[2,152,1792]{2,1,0:T(8,128)}, f32[2,152,1792]{2,1,0:T(8,128)}) fusion(f32[2,152,1792]{2,1,0:T(8,128)S(1)} %copy-done.47, bf16[2,152,1792]{2,1,0:T(8,128)(2,1)} %bitcast.173, f32[2,152,1792]{2,1,0:T(8,128)S(1)} %copy-done.62, f32[2,152,1792]{2,1,0:T(8,128)S(1)} %copy-done.63), kind=kLoop, calls=%fused_computation.234 | loop fusion | flops 9261056 | bytes 15253504 | tf_op jit(solution)/shard_map/convert_element_type | solution.py:33
  452.2 7.4 %collective-permute-done.58 = f32[2,1792]{1,0:T(2,128)S(1)} collective-permute-done((f32[2,1792]{1,0:T(2,128)S(1)}, f32[2,1792]{1,0:T(2,128)S(1)}, u32[]{:S(2)}, u32[]{:S(2)}) %collective-permute-start.58) | collective-permute-done | bytes 14368 | tf_op jit(solution)/shard_map/ppermute | solution.py:190
  (515 shorter events, 238.1 us)
Async XLA Ops:
  7.2 65.9 %all-gather.3.cloned.1.call-start = ((), (), s32[]{:S(2)}) async-start(), calls=%async_computation.3 | async-start | bytes 3440640 | tf_op jit(solution)/shard_map/all_gather | solution.py:593
  9.9 180.3 %all-gather.5.cloned.1.call-start = ((), (), s32[]{:S(2)}) async-start(), calls=%async_computation.4 | async-start | bytes 8171520 | tf_op jit(solution)/shard_map/all_gather | solution.py:596
  16.7 297.3 %reduce-scatter.6.cloned.1.call-start = ((), (), s32[]{:S(2)}) async-start(), calls=%async_computation.5 | async-start | bytes 2723840 | tf_op jit(solution)/shard_map/reduce_scatter | solution.py:715
  43.5 25.3 %collective-permute-start.6 = (bf16[256,1792]{1,0:T(8,128)(2,1)}, bf16[256,1792]{1,0:T(8,128)(2,1)}, u32[]{:S(2)}, u32[]{:S(2)}) collective-permute-start(bf16[256,1792]{1,0:T(8,128)(2,1)} %get-tuple-element.386), channel_id=1, source_target_pairs={{0,1},{1,0},{2,3},{3,2},{4,5},{5,4},{6,7},{7,6},{8,9},{9,8},{10,11... | collective-permute-start | bytes 2752520 | tf_op jit(solution)/shard_map/ppermute | solution.py:152
  43.6 20.4 %collective-permute-start.8 = (bf16[128,1792]{1,0:T(8,128)(2,1)S(1)}, bf16[128,1792]{1,0:T(8,128)(2,1)}, u32[]{:S(2)}, u32[]{:S(2)}) collective-permute-start(bf16[128,1792]{1,0:T(8,128)(2,1)S(1)} %get-tuple-element.145), channel_id=1, source_target_pairs={{0,2},{1,5},{2,0},{3,7},{4,6},{5,1},{6,4},{7,3},{8,10},{9,13},{10,... | collective-permute-start | bytes 1376264 | tf_op jit(solution)/shard_map/ppermute | solution.py:145
  65.1 19.7 %collective-permute-start.10 = (bf16[256,1792]{1,0:T(8,128)(2,1)S(1)}, bf16[256,1792]{1,0:T(8,128)(2,1)S(1)}, u32[]{:S(2)}, u32[]{:S(2)}) collective-permute-start(bf16[256,1792]{1,0:T(8,128)(2,1)S(1)} %constant_dynamic-update-slice_fusion.7.refs_4_.refs_2_), channel_id=1, source_target_pairs={{0,4},{1,3},{2,6},{3,1},{4,0},{5,7},{6,2},{7,5},{8,12},{9,11},{10,... | collective-permute-start | bytes 2752520 | tf_op jit(solution)/shard_map/ppermute | solution.py:151
  103.0 54.7 %collective-permute-start.23 = (bf16[256,1792]{1,0:T(8,128)(2,1)S(1)}, bf16[256,1792]{1,0:T(8,128)(2,1)S(1)}, u32[]{:S(2)}, u32[]{:S(2)}) collective-permute-start(bf16[256,1792]{1,0:T(8,128)(2,1)S(1)} %constant_dynamic-update-slice_fusion.14.refs_4_.refs_6_), channel_id=1, source_target_pairs={{0,1},{1,0},{2,3},{3,2},{4,5},{5,4},{6,7},{7,6},{8,9},{9,8},{10,11... | collective-permute-start | bytes 2752520 | tf_op jit(solution)/shard_map/ppermute | solution.py:152
  103.1 24.3 %collective-permute-start.18 = (bf16[256,1792]{1,0:T(8,128)(2,1)S(1)}, bf16[256,1792]{1,0:T(8,128)(2,1)S(1)}, u32[]{:S(2)}, u32[]{:S(2)}) collective-permute-start(bf16[256,1792]{1,0:T(8,128)(2,1)S(1)} %constant_dynamic-update-slice_fusion.14.refs_4_.refs_6_), channel_id=1, source_target_pairs={{0,4},{1,3},{2,6},{3,1},{4,0},{5,7},{6,2},{7,5},{8,12},{9,11},{10,... | collective-permute-start | bytes 2752520 | tf_op jit(solution)/shard_map/ppermute | solution.py:151
  103.7 22.7 %collective-permute-start.11 = (bf16[256,1792]{1,0:T(8,128)(2,1)S(1)}, bf16[256,1792]{1,0:T(8,128)(2,1)S(1)}, u32[]{:S(2)}, u32[]{:S(2)}) collective-permute-start(bf16[256,1792]{1,0:T(8,128)(2,1)S(1)} %fusion.10), channel_id=1, source_target_pairs={{0,4},{1,3},{2,6},{3,1},{4,0},{5,7},{6,2},{7,5},{8,12},{9,11},{10,... | collective-permute-start | bytes 2752520 | tf_op jit(solution)/shard_map/ppermute | solution.py:172
  105.4 35.7 %collective-permute-start.17 = (bf16[256,1792]{1,0:T(8,128)(2,1)S(1)}, bf16[256,1792]{1,0:T(8,128)(2,1)S(1)}, u32[]{:S(2)}, u32[]{:S(2)}) collective-permute-start(bf16[256,1792]{1,0:T(8,128)(2,1)S(1)} %fusion.9), channel_id=1, source_target_pairs={{0,4},{1,3},{2,6},{3,1},{4,0},{5,7},{6,2},{7,5},{8,12},{9,11},{10,... | collective-permute-start | bytes 2752520 | tf_op jit(solution)/shard_map/ppermute | solution.py:172
  127.4 30.4 %collective-permute-start.24 = (bf16[256,1792]{1,0:T(8,128)(2,1)S(1)}, bf16[256,1792]{1,0:T(8,128)(2,1)S(1)}, u32[]{:S(2)}, u32[]{:S(2)}) collective-permute-start(bf16[256,1792]{1,0:T(8,128)(2,1)S(1)} %collective-permute-done.18.refs_5_.refs_7_), channel_id=1, source_target_pairs={{0,1},{1,0},{2,3},{3,2},{4,5},{5,4},{6,7},{7,6},{8,9},{9,8},{10,11... | collective-permute-start | bytes 2752520 | tf_op jit(solution)/shard_map/ppermute | solution.py:156
  233.6 32.8 %collective-permute-start.33 = (bf16[256,1792]{1,0:T(8,128)(2,1)}, bf16[256,1792]{1,0:T(8,128)(2,1)}, u32[]{:S(2)}, u32[]{:S(2)}) collective-permute-start(bf16[256,1792]{1,0:T(8,128)(2,1)} %fusion.38), channel_id=1, source_target_pairs={{0,4},{1,3},{2,6},{3,1},{4,0},{5,7},{6,2},{7,5},{8,12},{9,11},{10,... | collective-permute-start | bytes 2752520 | tf_op jit(solution)/shard_map/ppermute | solution.py:172
  237.2 42.4 %collective-permute-start.32 = (bf16[256,1792]{1,0:T(8,128)(2,1)}, bf16[256,1792]{1,0:T(8,128)(2,1)}, u32[]{:S(2)}, u32[]{:S(2)}) collective-permute-start(bf16[256,1792]{1,0:T(8,128)(2,1)} %fusion.39), channel_id=1, source_target_pairs={{0,4},{1,3},{2,6},{3,1},{4,0},{5,7},{6,2},{7,5},{8,12},{9,11},{10,... | collective-permute-start | bytes 2752520 | tf_op jit(solution)/shard_map/ppermute | solution.py:172
  248.6 157.3 %reduce-scatter.8.cloned.1.call-start = ((), (), s32[]{:S(2)}) async-start(), calls=%async_computation.6 | async-start | bytes 5447680 | tf_op jit(solution)/shard_map/reduce_scatter | solution.py:715
  306.5 172.2 %reduce-scatter.10.cloned.1.call-start = ((), (), s32[]{:S(2)}) async-start(), calls=%async_computation.7 | async-start | bytes 3440640
  306.6 28.8 %collective-permute-start.37 = (bf16[2,256,1792]{2,1,0:T(8,128)(2,1)}, bf16[2,256,1792]{2,1,0:T(8,128)(2,1)}, u32[]{:S(2)}, u32[]{:S(2)}) collective-permute-start(bf16[2,256,1792]{2,1,0:T(8,128)(2,1)} %copy-done.24), channel_id=1, source_target_pairs={{0,1},{1,0},{2,3},{3,2},{4,5},{5,4},{6,7},{7,6},{8,9},{9,8},{10,11... | collective-permute-start | bytes 5505032 | tf_op jit(solution)/shard_map/ppermute | solution.py:165
  311.1 37.3 %collective-permute-start.44 = (bf16[256,1792]{1,0:T(8,128)(2,1)}, bf16[256,1792]{1,0:T(8,128)(2,1)}, u32[]{:S(2)}, u32[]{:S(2)}) collective-permute-start(bf16[256,1792]{1,0:T(8,128)(2,1)} %get-tuple-element.379), channel_id=1, source_target_pairs={{0,1},{1,0},{2,3},{3,2},{4,5},{5,4},{6,7},{7,6},{8,9},{9,8},{10,11... | collective-permute-start | bytes 2752520 | tf_op jit(solution)/shard_map/ppermute | solution.py:152
  311.2 24.2 %collective-permute-start.40 = (bf16[256,1792]{1,0:T(8,128)(2,1)}, bf16[256,1792]{1,0:T(8,128)(2,1)}, u32[]{:S(2)}, u32[]{:S(2)}) collective-permute-start(bf16[256,1792]{1,0:T(8,128)(2,1)} %get-tuple-element.379), channel_id=1, source_target_pairs={{0,4},{1,3},{2,6},{3,1},{4,0},{5,7},{6,2},{7,5},{8,12},{9,11},{10,... | collective-permute-start | bytes 2752520 | tf_op jit(solution)/shard_map/ppermute | solution.py:151
  334.4 52.1 %collective-permute-start.47 = (bf16[2,256,1792]{2,1,0:T(8,128)(2,1)}, bf16[2,256,1792]{2,1,0:T(8,128)(2,1)}, u32[]{:S(2)}, u32[]{:S(2)}) collective-permute-start(bf16[2,256,1792]{2,1,0:T(8,128)(2,1)} %bitcast.38), channel_id=1, source_target_pairs={{0,1},{1,0},{2,3},{3,2},{4,5},{5,4},{6,7},{7,6},{8,9},{9,8},{10,11... | collective-permute-start | bytes 5505032 | tf_op jit(solution)/shard_map/ppermute | solution.py:165
  337.8 52.5 %collective-permute-start.43 = (bf16[256,1792]{1,0:T(8,128)(2,1)}, bf16[256,1792]{1,0:T(8,128)(2,1)}, u32[]{:S(2)}, u32[]{:S(2)}) collective-permute-start(bf16[256,1792]{1,0:T(8,128)(2,1)} %fusion.40), channel_id=1, source_target_pairs={{0,4},{1,3},{2,6},{3,1},{4,0},{5,7},{6,2},{7,5},{8,12},{9,11},{10,... | collective-permute-start | bytes 2752520 | tf_op jit(solution)/shard_map/ppermute | solution.py:172
  367.4 21.6 %collective-permute-start.46 = (bf16[2,256,1792]{2,1,0:T(8,128)(2,1)}, bf16[2,256,1792]{2,1,0:T(8,128)(2,1)S(1)}, u32[]{:S(2)}, u32[]{:S(2)}) collective-permute-start(bf16[2,256,1792]{2,1,0:T(8,128)(2,1)} %bitcast.41), channel_id=1, source_target_pairs={{0,1},{1,0},{2,3},{3,2},{4,5},{5,4},{6,7},{7,6},{8,9},{9,8},{10,11... | collective-permute-start | bytes 5505032 | tf_op jit(solution)/shard_map/ppermute | solution.py:165
  399.3 25.6 %collective-permute-start.49 = (bf16[2,256,1792]{2,1,0:T(8,128)(2,1)}, bf16[2,256,1792]{2,1,0:T(8,128)(2,1)}, u32[]{:S(2)}, u32[]{:S(2)}) collective-permute-start(bf16[2,256,1792]{2,1,0:T(8,128)(2,1)} %get-tuple-element.242), channel_id=1, source_target_pairs={{0,1},{1,0},{2,3},{3,2},{4,5},{5,4},{6,7},{7,6},{8,9},{9,8},{10,11... | collective-permute-start | bytes 5505032 | tf_op jit(solution)/shard_map/ppermute | solution.py:165
  403.5 30.3 %collective-permute-start.52 = (bf16[256,1792]{1,0:T(8,128)(2,1)}, bf16[256,1792]{1,0:T(8,128)(2,1)}, u32[]{:S(2)}, u32[]{:S(2)}) collective-permute-start(bf16[256,1792]{1,0:T(8,128)(2,1)} %fusion.4), channel_id=1, source_target_pairs={{0,4},{1,3},{2,6},{3,1},{4,0},{5,7},{6,2},{7,5},{8,12},{9,11},{10,... | collective-permute-start | bytes 2752520 | tf_op jit(solution)/shard_map/ppermute | solution.py:172
  446.0 20.2 %collective-permute-start.51 = (bf16[256,1792]{1,0:T(8,128)(2,1)S(1)}, bf16[256,1792]{1,0:T(8,128)(2,1)S(1)}, u32[]{:S(2)}, u32[]{:S(2)}) collective-permute-start(bf16[256,1792]{1,0:T(8,128)(2,1)S(1)} %fusion.41), channel_id=1, source_target_pairs={{0,4},{1,3},{2,6},{3,1},{4,0},{5,7},{6,2},{7,5},{8,12},{9,11},{10,... | collective-permute-start | bytes 2752520 | tf_op jit(solution)/shard_map/ppermute | solution.py:172
  (159 other events, 1189.1 us)
Sparse Core Ops, SparseCore 0:
  10.2 59.6 all-gather.2
  72.0 118.0 all-gather.4
  248.7 44.6 reduce-scatter.5
  306.6 78.5 reduce-scatter.7
  425.0 53.5 reduce-scatter.9

commit v2 on v1

--- a/solution.py
+++ b/solution.py
@@ -192,13 +192,13 @@
     return tensor
 
 
-def head_parts(feat_dim, head_dim, inv_ref, proj_ref, taps_ref, link_ref, p_ref):
+def head_parts(feat_dim, head_dim, inv_ref, proj_ref, proj_cols, taps, link_ref, p_ref):
     length = p_ref.shape[0]
     chunks = inv_ref.shape[0]
     rows = length // chunks
     for chunk in range(chunks):
         source = pl.multiple_of(inv_ref[chunk] * rows, rows)
-        p_ref[chunk * rows : (chunk + 1) * rows, :] = proj_ref[pl.ds(source, rows), :]
+        p_ref[chunk * rows : (chunk + 1) * rows, :] = proj_ref[pl.ds(source, rows), proj_cols]
     packed = p_ref[...]
     pack_dim = packed.shape[1]
     lane = lax.broadcasted_iota(jnp.int32, (length, LANES), 1)
@@ -209,7 +209,6 @@
     inner = jnp.where(lane < head_dim, inner, 0.0)
     gate = pltpu.roll(packed, pack_dim - 2 * feat_dim - head_dim, 1)[:, :LANES]
     gate = jnp.where(lane < head_dim, gate, 0.0)
-    taps = taps_ref[0]
     shifted = [inner]
     conv = taps[0:1, :] * inner
     for offset in range(1, taps.shape[0]):
@@ -234,7 +233,7 @@
     feat_dim, head_dim, inv_ref, proj_ref, taps_ref, link_ref, segc_ref, segr_ref, out_ref, p_ref
 ):
     queries, keys, gate, taps, shifted, conv = head_parts(
-        feat_dim, head_dim, inv_ref, proj_ref, taps_ref, link_ref, p_ref
+        feat_dim, head_dim, inv_ref, proj_ref, slice(None), taps_ref[0], link_ref, p_ref
     )
     length = p_ref.shape[0]
     values = low(conv * (gate * jax.nn.sigmoid(gate))).T
@@ -253,79 +252,98 @@
         out_ref[pl.ds(target, rows), :] = attended[chunk * rows : (chunk + 1) * rows]
 
 
-def backward_kernel(
-    feat_dim,
-    head_dim,
-    inv_ref,
-    proj_ref,
-    grad_ref,
-    taps_ref,
-    link_ref,
-    segc_ref,
-    segr_ref,
-    out_ref,
-    tap_ref,
-    p_ref,
-    g_ref,
-    dk_ref,
-    dv_ref,
-):
-    queries, keys, gate, taps, shifted, conv = head_parts(
-        feat_dim, head_dim, inv_ref, proj_ref, taps_ref, link_ref, p_ref
-    )
+def backward_kernel(feat_dim, head_dim, has_earlier, inv_ref, *refs):
+    block_refs, refs = refs[:4], refs[4:]
+    normed_ref, proj_ref, att_ref, weight_ref, taps_ref, link_ref, segc_ref, segr_ref = refs[:8]
+    earlier_ref, refs = (refs[8], refs[9:]) if has_earlier else (None, refs[8:])
+    own_ref, other_ref, sum_ref, tap_ref = refs[:4]
+    p_ref, g_ref, dk_ref, dv_ref, resid_ref, att_grad_ref, packed_ref = refs[4:]
+    heads = taps_ref.shape[0]
     length = p_ref.shape[0]
+    pack_dim = p_ref.shape[1]
+    packs = heads * pack_dim
     chunks = inv_ref.shape[0]
     rows = length // chunks
-    for chunk in range(chunks):
-        source = pl.multiple_of(inv_ref[chunk] * rows, rows)
-        g_ref[chunk * rows : (chunk + 1) * rows, :] = grad_ref[pl.ds(source, rows), :]
-    grad = g_ref[...]
-    sigmoid_val = jax.nn.sigmoid(gate)
-    gate_act = gate * sigmoid_val
-    values = low(conv * gate_act)
-    keys_turned = keys.T
+    block_rows = length // 4
+    for block, ref in enumerate(block_refs):
+        resid_ref[block * block_rows : (block + 1) * block_rows, :] = ref[...]
+    att_grad_ref[...] = low(dot_nn(resid_ref[...], weight_ref[:, packs:]))
     root = 1.0 / math.sqrt(feat_dim)
-    dk_ref[...] = jnp.zeros_like(dk_ref)
-    dv_ref[...] = jnp.zeros_like(dv_ref)
-    query_grads = []
-    for block in range(length // BLOCK_T):
-        first, last = block * BLOCK_T, (block + 1) * BLOCK_T
-        score, kept, probs, scale = kept_scores(
-            feat_dim, block, keys, queries, segc_ref, segr_ref
-        )
-        weight_grad = dot_nt(values[:last], grad[first:last])
-        row_dot = jnp.sum(weight_grad * probs, axis=0, keepdims=True)
-        score_grad = low(
-            jnp.where(kept, (weight_grad - row_dot) * scale * (1.0 + score), 0.0)
-        )
-        query_grads.append(dot_nn(keys_turned[:, :last], score_grad).T)
-        dk_ref[:last, :] += dot_nn(score_grad, queries[first:last])
-        dv_ref[:last, :] += dot_nn(low(probs), grad[first:last])
-    grad_queries = jnp.concatenate(query_grads, axis=0) * root
-    grad_keys = dk_ref[...] * root
-    grad_values = dv_ref[...]
-    grad_conv = grad_values * gate_act
-    grad_gate = grad_values * conv * (sigmoid_val * (1.0 + gate * (1.0 - sigmoid_val)))
-    grad_inner = taps[0:1, :] * grad_conv
-    tap_rows = [jnp.sum(grad_conv * shifted[0], axis=0, keepdims=True)]
-    for offset in range(1, taps.shape[0]):
-        masked = grad_conv * link_ref[:, offset : offset + 1]
-        tap_rows.append(jnp.sum(masked * shifted[offset], axis=0, keepdims=True))
-        grad_inner = grad_inner + taps[offset : offset + 1, :] * pltpu.roll(
-            masked, length - offset, 0
-        )
-    for offset, tap_row in enumerate(tap_rows):
-        tap_ref[0, offset : offset + 1, :] = tap_row
-    empty = jnp.zeros((length, LANES), jnp.float32)
-    packed = jnp.concatenate([grad_queries + pltpu.roll(grad_keys, feat_dim, 1), empty], axis=1)
-    packed = packed + pltpu.roll(jnp.concatenate([grad_inner, empty], axis=1), 2 * feat_dim, 1)
-    packed = low(
-        packed
-        + pltpu.roll(jnp.concatenate([grad_gate, empty], axis=1), 2 * feat_dim + head_dim, 1)
-    )
-    for chunk in range(chunks):
-        target = pl.multiple_of(inv_ref[chunk] * rows, rows)
-        out_ref[pl.ds(target, rows), :] = packed[chunk * rows : (chunk + 1) * rows]
+    for head in range(heads):
+        proj_cols = slice(head * pack_dim, (head + 1) * pack_dim)
+        queries, keys, gate, taps, shifted, conv = head_parts(
+            feat_dim, head_dim, inv_ref, proj_ref, proj_cols, taps_ref[head], link_ref, p_ref
+        )
+        for chunk in range(chunks):
+            source = pl.multiple_of(inv_ref[chunk] * rows, rows)
+            g_ref[chunk * rows : (chunk + 1) * rows, :] = att_grad_ref[
+                pl.ds(source, rows), head * LANES : (head + 1) * LANES
+            ]
+        grad = g_ref[...]
+        sigmoid_val = jax.nn.sigmoid(gate)
+        gate_act = gate * sigmoid_val
+        values = low(conv * gate_act)
+        keys_turned = keys.T
+        dk_ref[...] = jnp.zeros_like(dk_ref)
+        dv_ref[...] = jnp.zeros_like(dv_ref)
+        query_grads = []
+        for block in range(length // BLOCK_T):
+            first, last = block * BLOCK_T, (block + 1) * BLOCK_T
+            score, kept, probs, scale = kept_scores(
+                feat_dim, block, keys, queries, segc_ref, segr_ref
+            )
+            weight_grad = dot_nt(values[:last], grad[first:last])
+            row_dot = jnp.sum(weight_grad * probs, axis=0, keepdims=True)
+            score_grad = low(
+                jnp.where(kept, (weight_grad - row_dot) * scale * (1.0 + score), 0.0)
+            )
+            query_grads.append(dot_nn(keys_turned[:, :last], score_grad).T)
+            dk_ref[:last, :] += dot_nn(score_grad, queries[first:last])
+            dv_ref[:last, :] += dot_nn(low(probs), grad[first:last])
+        grad_queries = jnp.concatenate(query_grads, axis=0) * root
+        grad_keys = dk_ref[...] * root
+        grad_values = dv_ref[...]
+        grad_conv = grad_values * gate_act
+        grad_gate = grad_values * conv * (sigmoid_val * (1.0 + gate * (1.0 - sigmoid_val)))
+        grad_inner = taps[0:1, :] * grad_conv
+        tap_rows = [jnp.sum(grad_conv * shifted[0], axis=0, keepdims=True)]
+        for offset in range(1, taps.shape[0]):
+            masked = grad_conv * link_ref[:, offset : offset + 1]
+            tap_rows.append(jnp.sum(masked * shifted[offset], axis=0, keepdims=True))
+            grad_inner = grad_inner + taps[offset : offset + 1, :] * pltpu.roll(
+                masked, length - offset, 0
+            )
+        for offset, tap_row in enumerate(tap_rows):
+            tap_ref[head, offset : offset + 1, :] = tap_row
+        empty = jnp.zeros((length, LANES), jnp.float32)
+        packed = jnp.concatenate(
+            [grad_queries + pltpu.roll(grad_keys, feat_dim, 1), empty], axis=1
+        )
+        packed = packed + pltpu.roll(
+            jnp.concatenate([grad_inner, empty], axis=1), 2 * feat_dim, 1
+        )
+        packed = low(
+            packed
+            + pltpu.roll(jnp.concatenate([grad_gate, empty], axis=1), 2 * feat_dim + head_dim, 1)
+        )
+        for chunk in range(chunks):
+            target = pl.multiple_of(inv_ref[chunk] * rows, rows)
+            packed_ref[pl.ds(target, rows), proj_cols] = packed[chunk * rows : (chunk + 1) * rows]
+    for block in range(4):
+        ref = (own_ref, other_ref)[block // 2]
+        ref[block % 2] = low(
+            dot_nt(
+                packed_ref[block * block_rows : (block + 1) * block_rows, :],
+                weight_ref[:, :packs],
+            )
+        )
+    mix_sum = dot_tn(normed_ref[...], packed_ref[...])
+    out_sum = dot_tn(resid_ref[...], att_ref[...])
+    if has_earlier:
+        mix_sum = mix_sum + wide(earlier_ref[:, :packs])
+        out_sum = out_sum + wide(earlier_ref[:, packs:])
+    sum_ref[:, :packs] = low(mix_sum)
+    sum_ref[:, packs:] = low(out_sum)
 
 
 def whole_spec(shape):
@@ -361,45 +379,42 @@
     )(inv, projected, taps, links, segc, segr)
 
 
-def attend_back(inv, projected, grad, taps, links, segc, segr, feat_dim, head_dim):
-    length = projected.shape[0]
+def attend_back(
+    inv, blocks, normed, projected, attended, weights, taps, links, segc, segr, earlier, sizes
+):
+    length, width = normed.shape
     heads, tap_count = taps.shape[0], taps.shape[1]
     pack_dim = projected.shape[1] // heads
+    operands = [*blocks, normed, projected, attended, weights, taps, links, segc, segr]
+    operands += [] if earlier is None else [earlier]
+    half = jax.ShapeDtypeStruct((2, length // 4, width), jnp.bfloat16)
+    vmem = pl.BlockSpec(memory_space=pltpu.VMEM)
     return pl.pallas_call(
-        functools.partial(backward_kernel, feat_dim, head_dim),
+        functools.partial(backward_kernel, *sizes, earlier is not None),
+        in_specs=[pl.BlockSpec(memory_space=pltpu.SMEM)] + [vmem] * len(operands),
+        out_specs=(vmem,) * 4,
         out_shape=(
-            jax.ShapeDtypeStruct((length, heads * pack_dim), jnp.bfloat16),
+            half,
+            half,
+            jax.ShapeDtypeStruct(weights.shape, jnp.bfloat16),
             jax.ShapeDtypeStruct((heads, tap_count, LANES), jnp.float32),
         ),
-        grid_spec=pltpu.PrefetchScalarGridSpec(
-            num_scalar_prefetch=1,
-            grid=(heads,),
-            in_specs=[
-                pl.BlockSpec((length, pack_dim), lambda head, inv: (0, head)),
-                pl.BlockSpec((length, LANES), lambda head, inv: (0, head)),
-                pl.BlockSpec((1, tap_count, LANES), lambda head, inv: (head, 0, 0)),
-                whole_spec(links.shape),
-                whole_spec(segc.shape),
-                whole_spec(segr.shape),
-            ],
-            out_specs=(
-                pl.BlockSpec((length, pack_dim), lambda head, inv: (0, head)),
-                pl.BlockSpec((1, tap_count, LANES), lambda head, inv: (head, 0, 0)),
-            ),
-            scratch_shapes=[
-                pltpu.VMEM((length, pack_dim), jnp.float32),
-                pltpu.VMEM((length, LANES), jnp.bfloat16),
-                pltpu.VMEM((length, LANES), jnp.float32),
-                pltpu.VMEM((length, LANES), jnp.float32),
-            ],
-        ),
-        compiler_params=pltpu.CompilerParams(vmem_limit_bytes=48 * 1024 * 1024),
+        scratch_shapes=[
+            pltpu.VMEM((length, pack_dim), jnp.float32),
+            pltpu.VMEM((length, LANES), jnp.bfloat16),
+            pltpu.VMEM((length, LANES), jnp.float32),
+            pltpu.VMEM((length, LANES), jnp.float32),
+            pltpu.VMEM((length, width), jnp.bfloat16),
+            pltpu.VMEM((length, heads * LANES), jnp.bfloat16),
+            pltpu.VMEM((length, heads * pack_dim), jnp.bfloat16),
+        ],
+        compiler_params=pltpu.CompilerParams(vmem_limit_bytes=56 * 1024 * 1024),
         cost_estimate=pl.CostEstimate(
-            flops=heads * length * length * LANES * 6,
-            bytes_accessed=heads * length * (pack_dim * 6 + LANES * 2),
+            flops=heads * length * (length * LANES * 6 + 6 * width * (pack_dim + LANES)),
+            bytes_accessed=10 * length * width,
             transcendentals=heads * length * LANES,
         ),
-    )(inv, projected, grad, taps, links, segc, segr)
+    )(inv, *operands)
 
 
 def ffn_kernel(*refs):
@@ -715,28 +730,37 @@
         return lax.psum_scatter(grads, "row", scatter_dimension=0, tiled=True)
 
     red_down = ffn_grads(cots, 2, 1)
-    red_up = ffn_grads(normed_two, 0, 2)
+    red_gate = ffn_grads(normed_two, 0, 1)
+    red_up = ffn_grads(normed_two, 1, 1)
     advance(back_a)
     low_a, gain_part = end_back(first, back_a)
     gain_two_sum = gain_two_sum + gain_part
     advance(back_b, low_a)
     low_b, gain_part = end_back(second, back_b)
     gain_two_sum = gain_two_sum + gain_part
-    sum_a = start_ffn_sum(first)
     advance(low_a, low_b)
 
-    projected_grads, resid_low, grads_input = [[None] * micro_count for _ in range(3)]
+    grads_input = [None] * micro_count
     tap_parts = [None] * micro_count
     gain_one_parts = [None] * micro_count
 
-    def start_attention_back(m, stage):
-        resid_low[m] = joined(finish(stage))
-        grad_att = low(dot_nn(resid_low[m], out_full))
-        grad_proj, tap_parts[m] = attend_back(
-            inv, projected[m], grad_att, taps, links[m], segc[m], segr[m], feat_dim, head_dim
-        )
-        projected_grads[m] = grad_proj
-        return col_scatter(*halves(lambda lo, hi: dot_nt(grad_proj[lo:hi], mix_full)))
+    def start_attention_back(m, stage, earlier):
+        blocks = line.hold(*finish(stage))
+        own, other, sums, tap_parts[m] = attend_back(
+            inv,
+            blocks,
+            normed_one[m],
+            projected[m],
+            attended[m],
+            mix_out,
+            taps,
+            links[m],
+            segc[m],
+            segr[m],
+            earlier,
+            (feat_dim, head_dim),
+        )
+        return col_scatter(own, other), sums
 
     def end_input(m, stage):
         back = finish(stage)
@@ -753,33 +777,25 @@
 
     (red_down,) = line.hold(red_down)
     line.mark(red_down)
-    input_a = start_attention_back(first, low_a)
-    advance(low_b, sum_a)
-    input_b = start_attention_back(second, low_b)
-    grad_projs = line.hold(*projected_grads)
-    grad_both = low(
-        jnp.concatenate(
-            [
-                sum(dot_tn(normed_one[m], grad_projs[m]) for m in micros),
-                sum(dot_tn(resid_low[m], attended[m]) for m in micros),
-            ],
-            axis=1,
-        )
-    )
-    line.mark(grad_both)
-    advance(input_a, input_b, sum_a)
+    input_a, sums = start_attention_back(first, low_a, None)
+    sum_a = start_ffn_sum(first)
+    advance(low_b)
+    (red_gate,) = line.hold(red_gate)
+    line.mark(red_gate)
+    input_b, sums = start_attention_back(second, low_b, sums)
     sum_b = start_ffn_sum(second)
-    red_up, grad_both = line.hold(red_up, grad_both)
-    line.mark(grad_both)
-    red_both = lax.psum_scatter(grad_both, "row", scatter_dimension=0, tiled=True)
+    advance(input_a, sum_a, input_b, sum_b)
+    red_up, sums = line.hold(red_up, sums)
+    line.mark(sums)
+    red_both = lax.psum_scatter(sums, "row", scatter_dimension=0, tiled=True)
+    advance(input_a, sum_a, input_b, sum_b)
+    end_input(first, input_a)
     end_ffn_sum(first, sum_a)
-    advance(input_a, sum_b, input_b)
-    end_input(first, input_a)
     end_input(second, input_b)
     end_ffn_sum(second, sum_b)
     red_both = wide(red_both)
     red_mix, red_out = red_both[:, : heads * pack_dim], red_both[:, heads * pack_dim :]
-    red_up = wide(red_up).reshape(2, hidden_own, width_all)
+    red_up = wide(jnp.stack([red_gate, red_up], axis=0))
     red_down = wide(red_down)
     gain_one_sum = sum(gain_one_parts)
     tap_sum = sum(tap_parts)

time: 501 us -> 491 us (0.980)
  Pallas kernels: 104 us -> 132 us
  local copies, waits for them, and re-layouts: 69.6 us -> 43 us
  matrix products: 33.2 us -> 6.79 us
  waiting for transfers between devices: 170 us -> 182 us
    pallas_call x2, Pallas kernels: 20.4 us -> 44.2 us  [attend_back(): pl.pallas_call(functools.partial(backward_kernel, *sizes, earlier is not...]
    unnamed x253 -> x209, local copies, waits for them, and re-layouts: 43.4 us -> 25 us
    ppermute x8, waiting for transfers between devices: 43.7 us -> 58.3 us  [scatter_col(): arrived = lax.ppermute(upper, 'col', chip_perm(col_count, last_step))]
    dot_general x4 -> x0, matrix products: 11.5 us -> none  [dot_tn(): lax.dot_general(left_side, right_side, (((0,), (0,)), ((), ())), preferre...]
    ppermute x7, waiting for transfers between devices: 16.2 us -> 6.3 us  [sum_over(): lax.ppermute(tensor, axis, [(i, i ^ bit) for i in range(count)])]
    ppermute x8, waiting for transfers between devices: 30.3 us -> 20.7 us  [scatter_col(): arrived = lax.ppermute(send, 'col', chip_perm(col_count, step))]
    ppermute x8, waiting for transfers between devices: 40.4 us -> 49.1 us  [gather_col(): arrived = lax.ppermute(held, 'col', chip_perm(col_count, 0))]
    dot_general x8 -> x4, matrix products: 11 us -> 2.68 us  [dot_nt(): lax.dot_general(left_side, right_side, (((1,), (1,)), ((), ())), preferre...]
  transfers between devices with their start and end apart: 68 -> 69, of which waited for: 28 -> 29; matrix products, arithmetic and copies ran while one was open for 26% -> 15% of each run, Pallas kernels for 17% -> 21%
where the time goes in v2:
time: 491 us; the launch traced here: 485 us
  waiting for transfers between devices  182 us (37%)
  Pallas kernels  132 us (27%)
  other arithmetic  53.1 us (11%)
  starting transfers between devices  52.1 us (11%)
  local copies, waits for them, and re-layouts  43 us (9%)
  between operations  15.9 us (3%)
  matrix products  6.79 us (1%)
    ppermute x8, waiting for transfers between devices, scatter_col(): arrived = lax.ppermute(upper, 'col', chip_perm(col_count, last_step))  58.3 us
    ppermute x8, waiting for transfers between devices, gather_col(): arrived = lax.ppermute(held, 'col', chip_perm(col_count, 0))  49.1 us
    pallas_call x2, Pallas kernels, attend_back(): pl.pallas_call(functools.partial(backward_kernel, *sizes, earlier is not...  44.2 us
    pallas_call x2, Pallas kernels, ffn_call(): pl.pallas_call(ffn_kernel, grid=(block_rows // rows,), in_specs=[block] *...  37.9 us
    ppermute x8, waiting for transfers between devices, gather_col(): arrived = lax.ppermute(held, 'col', chip_perm(col_count, step))  36.6 us
    convert_element_type x20, other arithmetic, low(): return tensor.astype(jnp.bfloat16)  32.1 us
    pallas_call x3, Pallas kernels, ffn_grad_call(): pl.pallas_call(functools.partial(ffn_grad_kernel, micro_count, 2), grid=(...  30.7 us
    unnamed x209, local copies, waits for them, and re-layouts  25 us
  transfers between devices with their start and end apart: 69, of which 29 were waited for; matrix products, arithmetic and copies ran while one was open for 15% of the time, Pallas kernels for 21%

profile of v2, /device:TPU:0, one launch (start us, length us, event | category | flops | bytes accessed | tf_op | source)
XLA Modules:
  0.0 485.4 jit_solution(15134444283883611950)
XLA Ops:
  26.4 10.9 %collective-permute-done.2 = bf16[128,1792]{1,0:T(8,128)(2,1)S(1)} collective-permute-done((bf16[128,1792]{1,0:T(8,128)(2,1)S(1)}, bf16[128,1792]{1,0:T(8,128)(2,1)S(1)}, u32[]{:S(2)}, u32[]{:S(2)}) %collective-permute-start.2) | collective-permute-done | bytes 458784 | tf_op jit(solution)/shard_map/ppermute | solution.py:145
  43.3 16.0 %collective-permute-done.5 = bf16[256,1792]{1,0:T(8,128)(2,1)} collective-permute-done((bf16[256,1792]{1,0:T(8,128)(2,1)}, bf16[256,1792]{1,0:T(8,128)(2,1)}, u32[]{:S(2)}, u32[]{:S(2)}) %collective-permute-start.5) | collective-permute-done | bytes 917536 | tf_op jit(solution)/shard_map/ppermute | solution.py:151
  76.2 6.1 %shard_map.397.refs_6_ = bf16[1024,256]{1,0:T(8,128)(2,1)S(1)} custom-call(s32[8]{0:T(128)S(1)} %dynamic-slice_bitcast_fusion.inv_ref, f32[1024,512]{1,0:T(8,128)S(1)} %fusion.80.proj_ref.refs_5_, f32[2,3,128]{2,1,0:T(4,128)S(1)} %pad.11.taps_ref.refs_8_, f32[1024,3]{1,0:T(8,128)S(1)} %copy.68.link_ref.refs_9_, s32[1024,1]{1,0:T(8,128)S(1)} %copy.69.segc_ref.refs_10_, ...), custom_call_target="tpu_custom_call" | custom-call | flops 805306368 | bytes 2621440 | tf_op jit(solution)/shard_map/pallas_call | solution.py:357
  85.3 6.0 %shard_map.398.refs_6_ = bf16[1024,256]{1,0:T(8,128)(2,1)S(1)} custom-call(s32[8]{0:T(128)S(1)} %dynamic-slice_bitcast_fusion.inv_ref, f32[1024,512]{1,0:T(8,128)S(1)} %fusion.81.proj_ref.refs_5_, f32[2,3,128]{2,1,0:T(4,128)S(1)} %pad.11.taps_ref.refs_8_, f32[1024,3]{1,0:T(8,128)S(1)} %copy.70.link_ref.refs_9_, s32[1024,1]{1,0:T(8,128)S(1)} %copy.71.segc_ref.refs_10_, ...), custom_call_target="tpu_custom_call" | custom-call | flops 805306368 | bytes 2621440 | tf_op jit(solution)/shard_map/pallas_call | solution.py:357
  95.3 6.3 %collective-permute-done.15 = bf16[128,1792]{1,0:T(8,128)(2,1)S(1)} collective-permute-done((bf16[128,1792]{1,0:T(8,128)(2,1)S(1)}, bf16[128,1792]{1,0:T(8,128)(2,1)S(1)}, u32[]{:S(2)}, u32[]{:S(2)}) %collective-permute-start.15) | collective-permute-done | bytes 458784 | tf_op jit(solution)/shard_map/ppermute | solution.py:145
  106.0 19.1 %collective-permute-done.11 = bf16[256,1792]{1,0:T(8,128)(2,1)S(1)} collective-permute-done((bf16[256,1792]{1,0:T(8,128)(2,1)S(1)}, bf16[256,1792]{1,0:T(8,128)(2,1)S(1)}, u32[]{:S(2)}, u32[]{:S(2)}) %collective-permute-start.11) | collective-permute-done | bytes 917536 | tf_op jit(solution)/shard_map/ppermute | solution.py:172
  126.1 13.7 %collective-permute-done.17 = bf16[256,1792]{1,0:T(8,128)(2,1)S(1)} collective-permute-done((bf16[256,1792]{1,0:T(8,128)(2,1)S(1)}, bf16[256,1792]{1,0:T(8,128)(2,1)S(1)}, u32[]{:S(2)}, u32[]{:S(2)}) %collective-permute-start.17) | collective-permute-done | bytes 917536 | tf_op jit(solution)/shard_map/ppermute | solution.py:172
  142.9 5.9 %collective-permute-done.20 = bf16[128,1792]{1,0:T(8,128)(2,1)S(1)} collective-permute-done((bf16[128,1792]{1,0:T(8,128)(2,1)S(1)}, bf16[128,1792]{1,0:T(8,128)(2,1)S(1)}, u32[]{:S(2)}, u32[]{:S(2)}) %collective-permute-start.20) | collective-permute-done | bytes 458784 | tf_op jit(solution)/shard_map/ppermute | solution.py:180
  155.8 12.0 %collective-permute-done.22 = bf16[128,1792]{1,0:T(8,128)(2,1)S(1)} collective-permute-done((bf16[128,1792]{1,0:T(8,128)(2,1)S(1)}, bf16[128,1792]{1,0:T(8,128)(2,1)S(1)}, u32[]{:S(2)}, u32[]{:S(2)}) %collective-permute-start.22) | collective-permute-done | bytes 458784 | tf_op jit(solution)/shard_map/ppermute | solution.py:145
  172.8 11.0 %collective-permute-done.28.refs_1_.refs_7_ = bf16[256,1792]{1,0:T(8,128)(2,1)} collective-permute-done((bf16[256,1792]{1,0:T(8,128)(2,1)S(1)}, bf16[256,1792]{1,0:T(8,128)(2,1)}, u32[]{:S(2)}, u32[]{:S(2)}) %collective-permute-start.28) | collective-permute-done | bytes 917536 | tf_op jit(solution)/shard_map/ppermute | solution.py:151
  183.9 6.4 %all-gather.5.cloned.1.call-done.refs_8_.weight_ref = bf16[3,608,1792]{2,1,0:T(8,128)(2,1)} async-done(((bf16[3,152,1792]{2,1,0:T(8,128)(2,1)}), bf16[3,608,1792]{2,1,0:T(8,128)(2,1)}) %all-gather.5.cloned.1.call-update) | async-done | bytes 6537232 | tf_op jit(solution)/shard_map/all_gather | solution.py:611
  190.3 18.9 %shard_map.399 = (bf16[3,608,1024]{2,1,0:T(8,128)(2,1)}, bf16[2,256,1792]{2,1,0:T(8,128)(2,1)}, bf16[2,256,1792]{2,1,0:T(8,128)(2,1)}) custom-call(bf16[256,1792]{1,0:T(8,128)(2,1)S(1)} %constant_dynamic-update-slice_fusion.16.refs_0_.refs_2_, bf16[256,1792]{1,0:T(8,128)(2,1)S(1)} %collective-permute-done.21.refs_1_.refs_3_, bf16[256,1792]{1,0:T(8,128)(2,1)} %copy-done.43, ...), custom_call_target="tpu_custom_call" | custom-call | flops 11156848640 | bytes 17547264 | tf_op jit(solution)/shard_map/pallas_call | solution.py:450
  209.3 19.1 %shard_map.400 = (bf16[3,608,1024]{2,1,0:T(8,128)(2,1)}, bf16[2,256,1792]{2,1,0:T(8,128)(2,1)}, bf16[2,256,1792]{2,1,0:T(8,128)(2,1)}) custom-call(bf16[256,1792]{1,0:T(8,128)(2,1)S(1)} %constant_dynamic-update-slice_fusion.18.refs_0_.refs_6_, bf16[256,1792]{1,0:T(8,128)(2,1)} %collective-permute-done.28.refs_1_.refs_7_, ...), custom_call_target="tpu_custom_call" | custom-call | flops 11156848640 | bytes 17547264 | tf_op jit(solution)/shard_map/pallas_call | solution.py:450
  233.9 10.2 %shard_map.401 = bf16[4,1,152,1792]{3,2,1,0:T(8,128)(2,1)} custom-call(bf16[3,608,1024]{2,1,0:T(8,128)(2,1)} %get-tuple-element.246.refs_0_.hidden_ref, bf16[3,608,1024]{2,1,0:T(8,128)(2,1)} %get-tuple-element.260.refs_1_.hidden_ref, bf16[256,1792]{1,0:T(8,128)(2,1)S(1)} %copy-done.15, bf16[256,1792]{1,0:T(8,128)(2,1)} %collective-permute-done.10.refs_5_.refs_3_, ...), custom_call_target="tpu_custom_call" | custom-call | flops 4462739456 | bytes 10764288 | tf_op jit(solution)/shard_map/pallas_call | solution.py:537
  246.3 10.0 %shard_map.402 = bf16[4,1,152,1792]{3,2,1,0:T(8,128)(2,1)} custom-call(bf16[3,608,1024]{2,1,0:T(8,128)(2,1)} %get-tuple-element.246.refs_0_.hidden_ref, bf16[3,608,1024]{2,1,0:T(8,128)(2,1)} %get-tuple-element.260.refs_1_.hidden_ref, bf16[256,1792]{1,0:T(8,128)(2,1)S(1)} %constant_dynamic-update-slice_fusion.16.refs_0_.refs_2_, ...), custom_call_target="tpu_custom_call" | custom-call | flops 4462739456 | bytes 10764288 | tf_op jit(solution)/shard_map/pallas_call | solution.py:537
  256.3 10.5 %shard_map.403 = bf16[4,1,152,1792]{3,2,1,0:T(8,128)(2,1)} custom-call(bf16[3,608,1024]{2,1,0:T(8,128)(2,1)} %get-tuple-element.246.refs_0_.hidden_ref, bf16[3,608,1024]{2,1,0:T(8,128)(2,1)} %get-tuple-element.260.refs_1_.hidden_ref, bf16[256,1792]{1,0:T(8,128)(2,1)S(1)} %constant_dynamic-update-slice_fusion.16.refs_0_.refs_2_, ...), custom_call_target="tpu_custom_call" | custom-call | flops 4462739456 | bytes 10764288 | tf_op jit(solution)/shard_map/pallas_call | solution.py:537
  271.7 6.9 %collective-permute-done.33 = bf16[128,1792]{1,0:T(8,128)(2,1)S(1)} collective-permute-done((bf16[128,1792]{1,0:T(8,128)(2,1)S(1)}, bf16[128,1792]{1,0:T(8,128)(2,1)S(1)}, u32[]{:S(2)}, u32[]{:S(2)}) %collective-permute-start.33) | collective-permute-done | bytes 458784 | tf_op jit(solution)/shard_map/ppermute | solution.py:180
  297.1 5.4 %collective-permute-done.36.refs_1_ = bf16[256,1792]{1,0:T(8,128)(2,1)} collective-permute-done((bf16[256,1792]{1,0:T(8,128)(2,1)S(1)}, bf16[256,1792]{1,0:T(8,128)(2,1)}, u32[]{:S(2)}, u32[]{:S(2)}) %collective-permute-start.36) | collective-permute-done | bytes 917536 | tf_op jit(solution)/shard_map/ppermute | solution.py:151
  306.1 6.2 %collective-permute-done.40 = bf16[128,1792]{1,0:T(8,128)(2,1)S(1)} collective-permute-done((bf16[128,1792]{1,0:T(8,128)(2,1)S(1)}, bf16[128,1792]{1,0:T(8,128)(2,1)S(1)}, u32[]{:S(2)}, u32[]{:S(2)}) %collective-permute-start.40) | collective-permute-done | bytes 458784 | tf_op jit(solution)/shard_map/ppermute | solution.py:145
  315.5 21.6 %shard_map.404 = (bf16[2,256,1792]{2,1,0:T(8,128)(2,1)}, bf16[2,256,1792]{2,1,0:T(8,128)(2,1)}, bf16[1792,768]{1,0:T(8,128)(2,1)}, f32[2,3,128]{2,1,0:T(4,128)}) custom-call(s32[8]{0:T(128)} %copy-done.21, bf16[256,1792]{1,0:T(8,128)(2,1)} %copy-done.76, bf16[256,1792]{1,0:T(8,128)(2,1)} %collective-permute-done.36.refs_1_, bf16[256,1792]{1,0:T(8,128)(2,1)} %copy-done.96, ...), custom_call_target="tpu_custom_call" | custom-call | flops 10066329600 | bytes 18350080 | tf_op jit(solution)/shard_map/pallas_call | solution.py:392
  347.6 22.6 %shard_map.406 = (bf16[2,256,1792]{2,1,0:T(8,128)(2,1)}, bf16[2,256,1792]{2,1,0:T(8,128)(2,1)}, bf16[1792,768]{1,0:T(8,128)(2,1)}, f32[2,3,128]{2,1,0:T(4,128)}) custom-call(s32[8]{0:T(128)} %copy-done.21, bf16[256,1792]{1,0:T(8,128)(2,1)} %constant_dynamic-update-slice_fusion.22.refs_0_, bf16[256,1792]{1,0:T(8,128)(2,1)} %collective-permute-done.43.refs_1_, ...), custom_call_target="tpu_custom_call" | custom-call | flops 10066329600 | bytes 18350080 | tf_op jit(solution)/shard_map/pallas_call | solution.py:392
  401.0 7.4 %fusion.67 = (bf16[2,152,1792]{2,1,0:T(8,128)(2,1)}, f32[2,152,1792]{2,1,0:T(8,128)}, f32[2,152,1792]{2,1,0:T(8,128)}, f32[2,152,1792]{2,1,0:T(8,128)}) fusion(f32[2,152,1792]{2,1,0:T(8,128)} %param.37, bf16[1,152,1792]{2,1,0:T(8,128)(2,1)} %bitcast.173, bf16[1,152,1792]{2,1,0:T(8,128)(2,1)S(1)} %bitcast.172, f32[2,152,1792]{2,1,0:T(8,128)} %param.39, ...), kind=kLoop, calls=%fused_computation.208 | loop fusion | flops 9805824 | bytes 15253504 | tf_op jit(solution)/shard_map/convert_element_type | solution.py:33
  415.6 11.0 %collective-permute-done.53 = bf16[256,1792]{1,0:T(8,128)(2,1)} collective-permute-done((bf16[256,1792]{1,0:T(8,128)(2,1)}, bf16[256,1792]{1,0:T(8,128)(2,1)}, u32[]{:S(2)}, u32[]{:S(2)}) %collective-permute-start.53) | collective-permute-done | bytes 917536 | tf_op jit(solution)/shard_map/ppermute | solution.py:172
  430.5 14.5 %collective-permute-done.52 = bf16[256,1792]{1,0:T(8,128)(2,1)} collective-permute-done((bf16[256,1792]{1,0:T(8,128)(2,1)}, bf16[256,1792]{1,0:T(8,128)(2,1)}, u32[]{:S(2)}, u32[]{:S(2)}) %collective-permute-start.52) | collective-permute-done | bytes 917536 | tf_op jit(solution)/shard_map/ppermute | solution.py:172
  (464 shorter events, 191.8 us)
Async XLA Ops:
  7.2 64.3 %all-gather.3.cloned.1.call-start = ((), (), s32[]{:S(2)}) async-start(), calls=%async_computation.4 | async-start | bytes 3440640 | tf_op jit(solution)/shard_map/all_gather | solution.py:608
  10.2 180.1 %all-gather.5.cloned.1.call-start = ((), (), s32[]{:S(2)}) async-start(), calls=%async_computation.5 | async-start | bytes 8171520 | tf_op jit(solution)/shard_map/all_gather | solution.py:611
  16.7 297.9 %reduce-scatter.5.cloned.1.call-start = ((), (), s32[]{:S(2)}) async-start(), calls=%async_computation.6 | async-start | bytes 2723840 | tf_op jit(solution)/shard_map/reduce_scatter | solution.py:730
  42.3 24.9 %collective-permute-start.6 = (bf16[256,1792]{1,0:T(8,128)(2,1)}, bf16[256,1792]{1,0:T(8,128)(2,1)}, u32[]{:S(2)}, u32[]{:S(2)}) collective-permute-start(bf16[256,1792]{1,0:T(8,128)(2,1)} %get-tuple-element.404), channel_id=1, source_target_pairs={{0,1},{1,0},{2,3},{3,2},{4,5},{5,4},{6,7},{7,6},{8,9},{9,8},{10,11... | collective-permute-start | bytes 2752520 | tf_op jit(solution)/shard_map/ppermute | solution.py:152
  101.7 54.1 %collective-permute-start.23 = (bf16[256,1792]{1,0:T(8,128)(2,1)S(1)}, bf16[256,1792]{1,0:T(8,128)(2,1)S(1)}, u32[]{:S(2)}, u32[]{:S(2)}) collective-permute-start(bf16[256,1792]{1,0:T(8,128)(2,1)S(1)} %constant_dynamic-update-slice_fusion.14.refs_4_.refs_6_), channel_id=1, source_target_pairs={{0,1},{1,0},{2,3},{3,2},{4,5},{5,4},{6,7},{7,6},{8,9},{9,8},{10,11... | collective-permute-start | bytes 2752520 | tf_op jit(solution)/shard_map/ppermute | solution.py:152
  101.7 24.4 %collective-permute-start.18 = (bf16[256,1792]{1,0:T(8,128)(2,1)S(1)}, bf16[256,1792]{1,0:T(8,128)(2,1)S(1)}, u32[]{:S(2)}, u32[]{:S(2)}) collective-permute-start(bf16[256,1792]{1,0:T(8,128)(2,1)S(1)} %constant_dynamic-update-slice_fusion.14.refs_4_.refs_6_), channel_id=1, source_target_pairs={{0,4},{1,3},{2,6},{3,1},{4,0},{5,7},{6,2},{7,5},{8,12},{9,11},{10,... | collective-permute-start | bytes 2752520 | tf_op jit(solution)/shard_map/ppermute | solution.py:151
  102.3 22.7 %collective-permute-start.11 = (bf16[256,1792]{1,0:T(8,128)(2,1)S(1)}, bf16[256,1792]{1,0:T(8,128)(2,1)S(1)}, u32[]{:S(2)}, u32[]{:S(2)}) collective-permute-start(bf16[256,1792]{1,0:T(8,128)(2,1)S(1)} %fusion.9), channel_id=1, source_target_pairs={{0,4},{1,3},{2,6},{3,1},{4,0},{5,7},{6,2},{7,5},{8,12},{9,11},{10,... | collective-permute-start | bytes 2752520 | tf_op jit(solution)/shard_map/ppermute | solution.py:172
  104.1 35.7 %collective-permute-start.17 = (bf16[256,1792]{1,0:T(8,128)(2,1)S(1)}, bf16[256,1792]{1,0:T(8,128)(2,1)S(1)}, u32[]{:S(2)}, u32[]{:S(2)}) collective-permute-start(bf16[256,1792]{1,0:T(8,128)(2,1)S(1)} %fusion.8), channel_id=1, source_target_pairs={{0,4},{1,3},{2,6},{3,1},{4,0},{5,7},{6,2},{7,5},{8,12},{9,11},{10,... | collective-permute-start | bytes 2752520 | tf_op jit(solution)/shard_map/ppermute | solution.py:172
  126.1 29.6 %collective-permute-start.24 = (bf16[256,1792]{1,0:T(8,128)(2,1)S(1)}, bf16[256,1792]{1,0:T(8,128)(2,1)S(1)}, u32[]{:S(2)}, u32[]{:S(2)}) collective-permute-start(bf16[256,1792]{1,0:T(8,128)(2,1)S(1)} %collective-permute-done.18.refs_5_.refs_7_), channel_id=1, source_target_pairs={{0,1},{1,0},{2,3},{3,2},{4,5},{5,4},{6,7},{7,6},{8,9},{9,8},{10,11... | collective-permute-start | bytes 2752520 | tf_op jit(solution)/shard_map/ppermute | solution.py:156
  244.1 102.0 %reduce-scatter.7.cloned.1.call-start = ((), (), s32[]{:S(2)}) async-start(), calls=%async_computation.7 | async-start | bytes 2723840 | tf_op jit(solution)/shard_map/reduce_scatter | solution.py:730
  244.2 22.8 %collective-permute-start.31 = (bf16[256,1792]{1,0:T(8,128)(2,1)}, bf16[256,1792]{1,0:T(8,128)(2,1)}, u32[]{:S(2)}, u32[]{:S(2)}) collective-permute-start(bf16[256,1792]{1,0:T(8,128)(2,1)} %fusion.37), channel_id=1, source_target_pairs={{0,4},{1,3},{2,6},{3,1},{4,0},{5,7},{6,2},{7,5},{8,12},{9,11},{10,... | collective-permute-start | bytes 2752520 | tf_op jit(solution)/shard_map/ppermute | solution.py:172
  245.7 36.1 %collective-permute-start.35 = (bf16[256,1792]{1,0:T(8,128)(2,1)S(1)}, bf16[256,1792]{1,0:T(8,128)(2,1)}, u32[]{:S(2)}, u32[]{:S(2)}) collective-permute-start(bf16[256,1792]{1,0:T(8,128)(2,1)S(1)} %fusion.38), channel_id=1, source_target_pairs={{0,4},{1,3},{2,6},{3,1},{4,0},{5,7},{6,2},{7,5},{8,12},{9,11},{10,... | collective-permute-start | bytes 2752520 | tf_op jit(solution)/shard_map/ppermute | solution.py:172
  256.3 144.4 %reduce-scatter.9.cloned.1.call-start = ((), (), s32[]{:S(2)}) async-start(), calls=%async_computation.8 | async-start | bytes 2723840 | tf_op jit(solution)/shard_map/reduce_scatter | solution.py:730
  288.8 25.7 %collective-permute-start.38 = (bf16[256,1792]{1,0:T(8,128)(2,1)S(1)}, bf16[256,1792]{1,0:T(8,128)(2,1)S(1)}, u32[]{:S(2)}, u32[]{:S(2)}) collective-permute-start(bf16[256,1792]{1,0:T(8,128)(2,1)S(1)} %constant_dynamic-update-slice_fusion.20.refs_0_), channel_id=1, source_target_pairs={{0,1},{1,0},{2,3},{3,2},{4,5},{5,4},{6,7},{7,6},{8,9},{9,8},{10,11... | collective-permute-start | bytes 2752520 | tf_op jit(solution)/shard_map/ppermute | solution.py:152
  313.0 33.1 %collective-permute-start.44 = (bf16[256,1792]{1,0:T(8,128)(2,1)}, bf16[256,1792]{1,0:T(8,128)(2,1)}, u32[]{:S(2)}, u32[]{:S(2)}) collective-permute-start(bf16[256,1792]{1,0:T(8,128)(2,1)} %constant_dynamic-update-slice_fusion.22.refs_0_), channel_id=1, source_target_pairs={{0,1},{1,0},{2,3},{3,2},{4,5},{5,4},{6,7},{7,6},{8,9},{9,8},{10,11... | collective-permute-start | bytes 2752520 | tf_op jit(solution)/shard_map/ppermute | solution.py:152
  313.0 31.8 %collective-permute-start.43 = (bf16[256,1792]{1,0:T(8,128)(2,1)}, bf16[256,1792]{1,0:T(8,128)(2,1)}, u32[]{:S(2)}, u32[]{:S(2)}) collective-permute-start(bf16[256,1792]{1,0:T(8,128)(2,1)} %constant_dynamic-update-slice_fusion.22.refs_0_), channel_id=1, source_target_pairs={{0,4},{1,3},{2,6},{3,1},{4,0},{5,7},{6,2},{7,5},{8,12},{9,11},{10,... | collective-permute-start | bytes 2752520 | tf_op jit(solution)/shard_map/ppermute | solution.py:151
  345.1 123.4 %reduce-scatter.11.cloned.1.call-start = ((), (), s32[]{:S(2)}) async-start(), calls=%async_computation.9 | async-start | bytes 3440640 | tf_op jit(solution)/shard_map/reduce_scatter | solution.py:790
  345.5 42.9 %collective-permute-start.41 = (bf16[2,256,1792]{2,1,0:T(8,128)(2,1)}, bf16[2,256,1792]{2,1,0:T(8,128)(2,1)}, u32[]{:S(2)}, u32[]{:S(2)}) collective-permute-start(bf16[2,256,1792]{2,1,0:T(8,128)(2,1)} %copy-done.22), channel_id=1, source_target_pairs={{0,1},{1,0},{2,3},{3,2},{4,5},{5,4},{6,7},{7,6},{8,9},{9,8},{10,11... | collective-permute-start | bytes 5505032 | tf_op jit(solution)/shard_map/ppermute | solution.py:165
  345.9 38.7 %collective-permute-start.42 = (bf16[2,256,1792]{2,1,0:T(8,128)(2,1)}, bf16[2,256,1792]{2,1,0:T(8,128)(2,1)}, u32[]{:S(2)}, u32[]{:S(2)}) collective-permute-start(bf16[2,256,1792]{2,1,0:T(8,128)(2,1)} %get-tuple-element.245), channel_id=1, source_target_pairs={{0,1},{1,0},{2,3},{3,2},{4,5},{5,4},{6,7},{7,6},{8,9},{9,8},{10,11... | collective-permute-start | bytes 5505032 | tf_op jit(solution)/shard_map/ppermute | solution.py:165
  390.7 22.4 %collective-permute-start.46 = (bf16[256,1792]{1,0:T(8,128)(2,1)}, bf16[256,1792]{1,0:T(8,128)(2,1)}, u32[]{:S(2)}, u32[]{:S(2)}) collective-permute-start(bf16[256,1792]{1,0:T(8,128)(2,1)} %fusion.40), channel_id=1, source_target_pairs={{0,4},{1,3},{2,6},{3,1},{4,0},{5,7},{6,2},{7,5},{8,12},{9,11},{10,... | collective-permute-start | bytes 2752520 | tf_op jit(solution)/shard_map/ppermute | solution.py:172
  397.1 29.5 %collective-permute-start.53 = (bf16[256,1792]{1,0:T(8,128)(2,1)}, bf16[256,1792]{1,0:T(8,128)(2,1)}, u32[]{:S(2)}, u32[]{:S(2)}) collective-permute-start(bf16[256,1792]{1,0:T(8,128)(2,1)} %fusion.41), channel_id=1, source_target_pairs={{0,4},{1,3},{2,6},{3,1},{4,0},{5,7},{6,2},{7,5},{8,12},{9,11},{10,... | collective-permute-start | bytes 2752520 | tf_op jit(solution)/shard_map/ppermute | solution.py:172
  400.0 45.0 %collective-permute-start.52 = (bf16[256,1792]{1,0:T(8,128)(2,1)}, bf16[256,1792]{1,0:T(8,128)(2,1)}, u32[]{:S(2)}, u32[]{:S(2)}) collective-permute-start(bf16[256,1792]{1,0:T(8,128)(2,1)} %fusion.42), channel_id=1, source_target_pairs={{0,4},{1,3},{2,6},{3,1},{4,0},{5,7},{6,2},{7,5},{8,12},{9,11},{10,... | collective-permute-start | bytes 2752520 | tf_op jit(solution)/shard_map/ppermute | solution.py:172
  411.9 36.3 %collective-permute-start.51 = (bf16[128,1792]{1,0:T(8,128)(2,1)S(1)}, bf16[128,1792]{1,0:T(8,128)(2,1)S(1)}, u32[]{:S(2)}, u32[]{:S(2)}) collective-permute-start(bf16[128,1792]{1,0:T(8,128)(2,1)S(1)} %slice.477), channel_id=1, source_target_pairs={{0,2},{1,5},{2,0},{3,7},{4,6},{5,1},{6,4},{7,3},{8,10},{9,13},{10,... | collective-permute-start | bytes 1376264 | tf_op jit(solution)/shard_map/ppermute | solution.py:180
  414.7 34.0 %collective-permute-start.50 = (bf16[128,1792]{1,0:T(8,128)(2,1)S(1)}, bf16[128,1792]{1,0:T(8,128)(2,1)S(1)}, u32[]{:S(2)}, u32[]{:S(2)}) collective-permute-start(bf16[128,1792]{1,0:T(8,128)(2,1)S(1)} %slice.476), channel_id=1, source_target_pairs={{0,2},{1,5},{2,0},{3,7},{4,6},{5,1},{6,4},{7,3},{8,10},{9,13},{10,... | collective-permute-start | bytes 1376264 | tf_op jit(solution)/shard_map/ppermute | solution.py:180
  (142 other events, 1441.8 us)
Sparse Core Ops, SparseCore 0:
  10.3 59.6 all-gather.2
  72.2 118.0 all-gather.4
  244.2 43.5 reduce-scatter.4
  290.6 44.7 reduce-scatter.6
  345.2 42.8 reduce-scatter.8
  400.8 53.9 reduce-scatter.10
